TPU v7x, 512 devices: a whole 4x8x8 slice. The times are simulated.
512 devices in a mesh: dp: 16 (over z_hi, y), cent: 32 (over x, z_lo, core).
Axes of the slice: x: 4, y: 8, z: 8 (z_hi: 2, z_lo: 4; z = z_hi * 4 + z_lo), core: 2. Of those that a mesh axis runs over, the one named last changes fastest.
Arguments:
- vectors: bfloat16 [131072, 1024], P(('dp', 'cent')), may hold values from -6 to 6
- candidates: int32 [131072, 4], P(('dp', 'cent')), may hold values from 0 to 31, all different within a row; in each aligned block of 256 rows (0 to 255, 256 to 511, ...) at most 64 rows name the same one
- centroids: bfloat16 [8192, 1024], P('cent', 'dp'), may hold values from -6 to 6
Outputs:
- new_centroids: float32 [8192, 1024], P('cent', 'dp')
- mass: float32 [8192], P('cent')
Inputs may be any that keep to these rules, and one draw needn't show every extreme that they name: `candidates`: each row names 4 different blocks. Within the 256 rows of one device (aligned blocks of rows, in order) no block is named by more than 64 rows, and some block by exactly 64. Every block is named by some row.
All inputs are finite; a program needn't handle non-finite values.
Results may differ from a plain program's by a relative error of at most 0.02.
The roundings to bfloat16 on the way count: a program that leaves them out, or rounds other values in their place, can miss the bound.
Values may be sent and summed in bfloat16 or wider, within the bound.
A program may use at most 64 MiB of HBM per device.

v0:
```python
import jax
import jax.numpy as jnp
from jax import lax
from jax.sharding import PartitionSpec as P

ITERS = 2


EPSILON = 1e-06
SHARPNESS = 20.0


def rms_unit(matrix):
    return matrix * lax.rsqrt(jnp.mean(matrix * matrix, axis=-1, keepdims=True) + EPSILON)


def body(vectors, candidates, centroids):
    cycle_size = lax.axis_size("cent")
    rows_here, features = vectors.shape
    per_row = candidates.shape[1]
    capacity = 2 * rows_here * per_row // cycle_size
    unit_vec = rms_unit(vectors.astype(jnp.float32)).astype(jnp.bfloat16)
    target_block = candidates.reshape(-1)
    onehot = (target_block[:, None] == jnp.arange(cycle_size, dtype=jnp.int32)[None, :]).astype(
        jnp.int32
    )
    position = jnp.sum((jnp.cumsum(onehot, axis=0) - 1) * onehot, axis=1)
    slot_index = target_block * capacity + position
    pair_ids = jnp.arange(rows_here * per_row, dtype=jnp.int32)
    slot_pair = jnp.full((cycle_size * capacity,), -1, jnp.int32).at[slot_index].set(pair_ids)
    slot_row = jnp.where(slot_pair >= 0, slot_pair // per_row, -1)
    send_rows = jnp.take(unit_vec, jnp.maximum(slot_row, 0), axis=0)
    send_rows = jnp.where((slot_row >= 0)[:, None], send_rows, jnp.zeros_like(send_rows))
    send_rows = send_rows.reshape(cycle_size, capacity, features)
    send_ids = slot_row.reshape(cycle_size, capacity)
    panel = centroids
    new_panel = None
    mass_total = None
    arrived_rows, arrived_ids = (
        lax.all_to_all(send_rows, "cent", split_axis=0, concat_axis=0, tiled=True),
        lax.all_to_all(send_ids, "cent", split_axis=0, concat_axis=0, tiled=True),
    )
    for sweep in range(ITERS):
        full_rows = lax.all_gather(panel, "dp", axis=1, tiled=True)
        unit_cent = rms_unit(full_rows.astype(jnp.float32)).astype(jnp.bfloat16)
        flat_rows = arrived_rows.reshape(-1, features)
        scores = lax.dot_general(
            flat_rows, unit_cent, (((1,), (1,)), ((), ())), preferred_element_type=jnp.float32
        )
        weights_raw = jnp.exp(scores * (SHARPNESS / features))
        partial_value = jnp.sum(weights_raw, axis=1).reshape(cycle_size, capacity)
        returned = lax.all_to_all(partial_value, "cent", split_axis=0, concat_axis=0, tiled=True)
        totals = jnp.sum(
            jnp.take(returned.reshape(-1), slot_index).reshape(rows_here, per_row), axis=1
        )
        send_totals = jnp.where(slot_row >= 0, jnp.take(totals, jnp.maximum(slot_row, 0)), 1.0)
        arrived_totals = lax.all_to_all(
            send_totals.reshape(cycle_size, capacity),
            "cent",
            split_axis=0,
            concat_axis=0,
            tiled=True,
        )
        live_flat = (arrived_ids >= 0).reshape(-1)
        totals_flat = jnp.where(live_flat, arrived_totals.reshape(-1), 1.0)
        shares = jnp.where(live_flat[:, None], weights_raw / totals_flat[:, None], 0.0)
        mass_part = jnp.sum(shares, axis=0)
        block_sums = lax.dot_general(
            shares.astype(jnp.bfloat16),
            flat_rows,
            (((0,), (0,)), ((), ())),
            preferred_element_type=jnp.float32,
        )
        sums_panel = lax.psum_scatter(
            block_sums.astype(jnp.bfloat16), "dp", scatter_dimension=1, tiled=True
        ).astype(jnp.float32)
        squares = jnp.sum(sums_panel * sums_panel, axis=1)
        squares, refine_mass_total = lax.psum((squares, mass_part), "dp")
        refine_new_panel = sums_panel * lax.rsqrt(squares / features + EPSILON)[:, None]
        new_panel = refine_new_panel
        mass_total = refine_mass_total
        panel = new_panel.astype(jnp.bfloat16)
    return (new_panel, mass_total)


def solution(mesh):
    return jax.shard_map(
        body,
        mesh=mesh,
        in_specs=(P(("dp", "cent"), None), P(("dp", "cent"), None), P("cent", "dp")),
        out_specs=(P("cent", "dp"), P("cent")),
        check_vma=False,
    )
```

profile of v0, /device:TPU:2, one launch (start us, length us, event | category | flops | bytes accessed | tf_op | source)
XLA Modules:
  0.0 858.4 jit_solution(7050871922978471674)
XLA Ops:
  9.0 9.0 %reduce-window.6 = s32[32,8,128]{2,1,0:T(8,128)S(1)} reduce-window(s32[32,8,128]{2,1,0:T(8,128)S(1)} %fusion.19, s32[]{:T(128)} %constant.50.clone.1), window={size=1x1x128 pad=0_0x0_0x127_0}, to_apply=%region_0.0 | reduce-window | flops 4161536 | bytes 262148 | tf_op jit(solution)/shard_map/reduce-window
  23.7 9.7 %gather_fusion = bf16[2048,1024]{1,0:T(8,128)(2,1)} fusion(bf16[256,1024]{1,0:T(8,128)(2,1)S(1)} %fusion.3, s32[2048]{0:T(1024)S(1)} %maximum_clamp_fusion), kind=kCustom, calls=%fused_computation.4 | custom fusion | bytes 8396800 | tf_op jit(solution)/shard_map/jit(_take)/gather | solution.py:32
  37.3 10.6 %all-to-all-start.1 = ((bf16[32,64,1024]{2,1,0:T(8,128)(2,1)}), bf16[32,64,1024]{2,1,0:T(8,128)(2,1)}, u32[]{:S(2)}, u32[]{:S(2)}) async-start(bf16[32,64,1024]{2,1,0:T(8,128)(2,1)} %select_select_fusion), calls=%async_computation.1 | async-start | bytes 8388608 | tf_op jit(solution)/shard_map/all_to_all | solution.py:40
  47.9 60.6 %all_gather.6 = bf16[256,1024]{0,1:T(8,128)(2,1)S(1)} all-gather(bf16[256,64]{0,1:T(8,128)(2,1)S(1)} %copy-done.1), channel_id=1, replica_groups=mesh['dp'=16,'cent'=32] {'dp'}, dimensions={1}, use_global_device_ids=true | all-gather | bytes 557056 | tf_op jit(solution)/shard_map/all_gather | solution.py:44
  108.7 43.7 %all-to-all-done.1 = bf16[32,64,1024]{2,1,0:T(8,128)(2,1)} async-done(((bf16[32,64,1024]{2,1,0:T(8,128)(2,1)}), bf16[32,64,1024]{2,1,0:T(8,128)(2,1)}, u32[]{:S(2)}, u32[]{:S(2)}) %all-to-all-start.1) | async-done | bytes 4194336 | tf_op jit(solution)/shard_map/all_to_all | solution.py:40
  152.4 4.9 fusion.31
  158.0 6.1 all-to-all-start.2
  164.7 5.8 all-to-all-done.2
  170.6 4.9 all-to-all-start
  176.8 6.1 gather_fusion.1
  183.2 13.2 %gather_fusion.2 = f32[2048]{0:T(1024)S(1)} fusion(f32[256]{0:T(256)S(1)} %reduce_sum.106, s32[2048]{0:T(1024)S(1)} %maximum_clamp_fusion), kind=kCustom, calls=%fused_computation.1.clone | custom fusion | bytes 24576 | tf_op jit(solution)/shard_map/jit(_take)/gather | solution.py:56
  197.1 7.8 all-to-all-start.3
  205.1 6.3 all-to-all-done.3
  212.2 5.4 convolution_convert_fusion.1
  217.7 216.2 %reduce-scatter.3.cloned.1.call-done = bf16[256,64]{0,1:T(8,128)(2,1)} async-done(((bf16[256,1024]{0,1:T(8,128)(2,1)}), bf16[256,64]{0,1:T(8,128)(2,1)}) %reduce-scatter.3.cloned.1.call-update) | async-done | bytes 32784 | tf_op jit(solution)/shard_map/reduce_scatter | solution.py:74
  434.7 49.0 %psum.21 = f32[256]{0:T(256)S(1)} all-reduce(f32[256]{0:T(256)S(1)} %fusion.20), channel_id=1, replica_groups=mesh['dp'=16,'cent'=32] {'dp'}, use_global_device_ids=true, to_apply=%region_10.13 | all-reduce | flops 256 | bytes 2048 | tf_op jit(solution)/shard_map/psum | solution.py:78
  484.4 47.9 %all_gather.7 = bf16[256,1024]{0,1:T(8,128)(2,1)S(1)} all-gather(bf16[256,64]{0,1:T(8,128)(2,1)S(1)} %fusion.21), channel_id=1, replica_groups=mesh['dp'=16,'cent'=32] {'dp'}, dimensions={1}, use_global_device_ids=true | all-gather | bytes 557056 | tf_op jit(solution)/shard_map/all_gather | solution.py:44
  536.2 12.9 %all_to_all.50 = f32[32,1,64]{2,1,0:T(1,128)S(1)} all-to-all(f32[32,1,64]{2,1,0:T(1,128)S(1)} %all_to_all.40), channel_id=1, replica_groups=mesh['dp'=16,'cent'=32] {'cent'}, dimensions={0} | all-to-all | bytes 16384 | tf_op jit(solution)/shard_map/all_to_all | solution.py:52
  549.9 6.1 gather_fusion.3
  556.3 13.2 %gather_fusion.4 = f32[2048]{0:T(1024)S(1)} fusion(f32[256]{0:T(256)S(1)} %reduce_sum.110, s32[2048]{0:T(1024)S(1)} %maximum_clamp_fusion), kind=kCustom, calls=%fused_computation.3.clone | custom fusion | bytes 24576 | tf_op jit(solution)/shard_map/jit(_take)/gather | solution.py:56
  569.6 10.7 %all_to_all.51 = f32[32,1,64]{2,1,0:T(1,128)S(1)} all-to-all(f32[32,1,64]{2,1,0:T(1,128)S(1)} %all_to_all.42), channel_id=1, replica_groups=mesh['dp'=16,'cent'=32] {'cent'}, dimensions={0} | all-to-all | bytes 16384 | tf_op jit(solution)/shard_map/all_to_all | solution.py:57
  581.0 4.8 convolution_convert_fusion
  586.1 213.8 %reduce-scatter.5.cloned.1.call-done = bf16[256,64]{0,1:T(8,128)(2,1)} async-done(((bf16[256,1024]{0,1:T(8,128)(2,1)}), bf16[256,64]{0,1:T(8,128)(2,1)}) %reduce-scatter.5.cloned.1.call-update) | async-done | bytes 32784 | tf_op jit(solution)/shard_map/reduce_scatter | solution.py:74
  800.7 49.5 %all-reduce = (f32[256]{0:T(256)S(1)}, f32[256]{0:T(256)}) all-reduce(f32[256]{0:T(256)S(1)} %fusion.22, f32[256]{0:T(256)S(1)} %fusion.12), channel_id=1, replica_groups=mesh['dp'=16,'cent'=32] {'dp'}, use_global_device_ids=true, to_apply=%region_16.19 | all-reduce | flops 512 | bytes 4096 | tf_op jit(solution)/shard_map/psum | solution.py:78
  (74 shorter events, 25.8 us)
Async XLA Ops:
  7.2 16.0 %copy-start = (bf16[256,1024]{1,0:T(8,128)(2,1)S(1)}, bf16[256,1024]{1,0:T(8,128)(2,1)}, u32[]{:S(2)}) copy-start(bf16[256,1024]{1,0:T(8,128)(2,1)} %param.7) | copy-start | bytes 1572868
  37.3 10.6 %copy-start.1 = (bf16[256,64]{0,1:T(8,128)(2,1)S(1)}, bf16[256,64]{0,1:T(8,128)(2,1)}, u32[]{:S(2)}) copy-start(bf16[256,64]{0,1:T(8,128)(2,1)} %param.9) | copy-start | bytes 98308
  37.3 115.1 %all-to-all-start.1 = ((bf16[32,64,1024]{2,1,0:T(8,128)(2,1)}), bf16[32,64,1024]{2,1,0:T(8,128)(2,1)}, u32[]{:S(2)}, u32[]{:S(2)}) async-start(bf16[32,64,1024]{2,1,0:T(8,128)(2,1)} %select_select_fusion), calls=%async_computation.1 | async-start | bytes 8388608 | tf_op jit(solution)/shard_map/all_to_all | solution.py:40
  158.0 12.6 %all-to-all-start.2 = ((f32[32,1,64]{2,1,0:T(1,128)}), f32[32,1,64]{2,1,0:T(1,128)S(1)}, u32[]{:S(2)}, u32[]{:S(2)}) async-start(f32[32,1,64]{2,1,0:T(1,128)} %all_to_all.36), calls=%async_computation.2 | async-start | bytes 32768 | tf_op jit(solution)/shard_map/all_to_all | solution.py:52
  170.6 26.6 %all-to-all-start = ((s32[32,1,64]{2,1,0:T(1,128)}), s32[32,1,64]{2,1,0:T(1,128)S(1)}, u32[]{:S(2)}, u32[]{:S(2)}) async-start(s32[32,1,64]{2,1,0:T(1,128)} %all_to_all.33), calls=%async_computation | async-start | bytes 32768 | tf_op jit(solution)/shard_map/all_to_all | solution.py:41
  197.1 14.3 %all-to-all-start.3 = ((f32[32,1,64]{2,1,0:T(1,128)}), f32[32,1,64]{2,1,0:T(1,128)S(1)}, u32[]{:S(2)}, u32[]{:S(2)}) async-start(f32[32,1,64]{2,1,0:T(1,128)} %all_to_all.38), calls=%async_computation.3 | async-start | bytes 32768 | tf_op jit(solution)/shard_map/all_to_all | solution.py:57
  204.9 229.0 %reduce-scatter.3.cloned.1.call-start = ((), (), s32[]{:S(2)}) async-start(), calls=%async_computation.8 | async-start | bytes 557056 | tf_op jit(solution)/shard_map/reduce_scatter | solution.py:74
  217.6 582.3 %reduce-scatter.5.cloned.1.call-start = ((), (), s32[]{:S(2)}) async-start(), calls=%async_computation.9 | async-start | bytes 557056 | tf_op jit(solution)/shard_map/reduce_scatter | solution.py:74
Sparse Core Ops, SparseCore 0:
  217.7 216.1 reduce-scatter.2
  585.9 213.9 reduce-scatter.4
where the time goes:
time: 859 us; the launch traced here: 858 us
  waiting for transfers between devices  486 us (57%)
  blocking collectives  231 us (27%)
  local copies, waits for them, and re-layouts  57.9 us (7%)
  starting transfers between devices  29.5 us (3%)
  other arithmetic  21.7 us (3%)
  matrix products  18.6 us (2%)
  between operations  14.4 us (2%)
    reduce_scatter x2, waiting for transfers between devices, body(): lax.psum_scatter(block_sums.astype(jnp.bfloat16), 'dp', scatter_dimension...  430 us
    all_gather x2, blocking collectives, body(): full_rows = lax.all_gather(panel, 'dp', axis=1, tiled=True)  109 us
    psum x2, blocking collectives, body(): squares, refine_mass_total = lax.psum((squares, mass_part), 'dp')  98.5 us
    all_to_all x1, waiting for transfers between devices, body(): lax.all_to_all(send_rows, 'cent', split_axis=0, concat_axis=0, tiled=True)  43.7 us
    gather x2, local copies, waits for them, and re-layouts, body(): jnp.take(totals, jnp.maximum(slot_row, 0))  26.4 us
  transfers between devices with their start and end apart: 6, of which 5 were waited for; matrix products, arithmetic and copies ran while one was open for 3% of the time, Pallas kernels for 0%

commit v1 on v0

v1 whole, which is shorter than its diff:
```python
import functools

import jax
import jax.numpy as jnp
from jax import lax
from jax.experimental import pallas as pl
from jax.experimental.pallas import tpu as pltpu
from jax.sharding import PartitionSpec as P

ITERS = 2
EPSILON = 1e-06
SHARPNESS = 20.0

D = 1024
ROWS = 256
BLOCK = 256
CAP = 64
N_DP = 16
N_CENT = 32
N_X = 4
N_Z = 4
LAYER = 8
SLOTS = N_CENT * CAP
PANEL = D // N_DP

F32 = jnp.float32
BF16 = jnp.bfloat16
MESH = pl.DeviceIdType.MESH


def cent_of(place):
    return ((place // 2) % N_X) * LAYER + (place // LAYER) * 2 + place % 2


def lanes(start, size):
    return pl.ds(pl.multiple_of(start, 128), size)


def kernel(
    vec_ref,
    cand_ref,
    cent_ref,
    out_ref,
    mass_ref,
    units,
    ranks,
    own_pick,
    packed,
    rows,
    raw,
    low,
    part,
    part_in,
    total,
    total_in,
    wide,
    unit_cent,
    panel_out,
    panel_in,
    fresh,
    edge_out,
    edge_in,
    z_send,
    z_recv,
    rank_send,
    rank_recv,
    x_send,
    x_recv,
    part_send,
    part_recv,
    total_send,
    total_recv,
    panel_send,
    panel_recv,
    fresh_send,
    fresh_recv,
    edge_send,
    edge_recv,
):
    dp = lax.axis_index("dp")
    cent = lax.axis_index("cent")
    x = cent // LAYER
    z = (cent // 2) % N_Z
    core = cent % 2
    here = z * LAYER + x * 2 + core

    def dp_peer(i):
        return lax.rem(dp + i, N_DP)

    def place_peer(i):
        return lax.rem(here + i, N_CENT)

    barrier = pltpu.get_barrier_semaphore()

    def greet_cent(i, carry):
        pl.semaphore_signal(
            barrier, inc=1, device_id=(dp, cent_of(place_peer(i))), device_id_type=MESH
        )
        return carry

    def greet_dp(i, carry):
        pl.semaphore_signal(barrier, inc=1, device_id=(dp_peer(i), cent), device_id_type=MESH)
        return carry

    lax.fori_loop(1, N_CENT, greet_cent, 0)
    lax.fori_loop(1, N_DP, greet_dp, 0)

    vec = vec_ref[...].astype(F32)
    vec_scale = lax.rsqrt(jnp.mean(vec * vec, axis=1, keepdims=True) + EPSILON)
    units[z] = (vec * vec_scale).astype(BF16)
    cand = cand_ref[...]
    place = lax.broadcasted_iota(jnp.int32, (N_CENT, ROWS), 0)
    block = ((place >> 1) & (N_X - 1)) * LAYER + (place >> 3) * 2 + (place & 1)
    named = cand[0:1, :] == block
    for j in range(1, cand.shape[0]):
        named = jnp.logical_or(named, cand[j : j + 1, :] == block)
    named_f = jnp.where(named, 1.0, 0.0)
    first = lax.broadcasted_iota(jnp.int32, (ROWS, ROWS), 0)
    second = lax.broadcasted_iota(jnp.int32, (ROWS, ROWS), 1)
    before = jnp.where(first < second, 1.0, 0.0).astype(BF16)
    rank = jnp.dot(named_f.astype(BF16), before, preferred_element_type=F32)
    slots = jnp.where(named, rank, -1.0).astype(jnp.int32)
    for layer in range(N_Z):
        ranks[layer, 0] = slots[layer * LAYER : (layer + 1) * LAYER]

    slot_iota = lax.broadcasted_iota(jnp.int32, (CAP, ROWS), 0)

    def pick_rows(rank_rows):
        picks = [
            jnp.where(rank_rows[j : j + 1, :] == slot_iota, 1.0, 0.0).astype(BF16)
            for j in range(LAYER)
        ]
        return jnp.concatenate(picks, axis=0)

    panel0 = cent_ref[...]
    half = BLOCK // 2
    fresh[0, dp] = jnp.concatenate([panel0[:half], panel0[half:]], axis=1)

    pl.semaphore_wait(barrier, N_CENT - 1 + N_DP - 1)

    def rank_copy(layer):
        return pltpu.make_async_remote_copy(
            src_ref=ranks.at[layer, 0],
            dst_ref=ranks.at[z, 1],
            send_sem=rank_send.at[layer],
            recv_sem=rank_recv.at[z],
            device_id=(dp, x * LAYER + layer * 2 + core),
            device_id_type=MESH,
        )

    def unit_copy(origin, side):
        return pltpu.make_async_remote_copy(
            src_ref=units.at[origin],
            dst_ref=units.at[origin],
            send_sem=z_send.at[origin, side],
            recv_sem=z_recv.at[origin],
            device_id=(dp, x * LAYER + (z + 2 * side - 1) * 2 + core),
            device_id_type=MESH,
        )

    def start_up(origin):
        @pl.when(z < N_Z - 1)
        def _():
            unit_copy(origin, 1).start()

    def start_down(origin):
        @pl.when(z > 0)
        def _():
            unit_copy(origin, 0).start()

    start_up(z)
    start_down(z)

    def send_rank(i, carry):
        rank_copy(lax.rem(z + i, N_Z)).start()
        return carry

    lax.fori_loop(1, N_Z, send_rank, 0)

    def fresh_copy(sweep, i):
        return pltpu.make_async_remote_copy(
            src_ref=fresh.at[sweep, dp],
            dst_ref=fresh.at[sweep, dp],
            send_sem=fresh_send.at[sweep],
            recv_sem=fresh_recv.at[sweep],
            device_id=(dp_peer(i), cent),
            device_id_type=MESH,
        )

    def send_fresh(sweep):
        def step(i, carry):
            fresh_copy(sweep, i).start()
            return carry

        lax.fori_loop(1, N_DP, step, 0)

    send_fresh(0)

    def row_copy(origin, i):
        target = lax.rem(x * 2 + core + i, LAYER)
        return pltpu.make_async_remote_copy(
            src_ref=packed.at[origin, target],
            dst_ref=rows.at[origin * LAYER + x * 2 + core],
            send_sem=x_send.at[origin, target],
            recv_sem=x_recv.at[origin * LAYER + x * 2 + core],
            device_id=(dp, (target // 2) * LAYER + z * 2 + target % 2),
            device_id_type=MESH,
        )

    def pack_and_send(origin, rank_rows):
        chosen = jnp.dot(pick_rows(rank_rows), units[origin], preferred_element_type=F32)
        packed[origin] = chosen.astype(BF16).reshape(LAYER, CAP, D)
        rows[origin * LAYER + x * 2 + core] = packed[origin, x * 2 + core]

        def step(i, carry):
            row_copy(origin, i).start()
            return carry

        lax.fori_loop(1, LAYER, step, 0)

    pack_and_send(z, ranks[z, 0])

    for layer in range(N_Z):
        own_pick[layer * LAYER * CAP : (layer + 1) * LAYER * CAP] = pick_rows(ranks[layer, 0])

    def event(e, carry):
        distance = (e + 1) // 2
        up = lax.rem(e, 2)
        origin = z + jnp.where(up == 1, -distance, distance)

        @pl.when(jnp.logical_and(origin >= 0, origin < N_Z))
        def _():
            unit_copy(origin, 0).wait_recv()

            @pl.when(up == 1)
            def _():
                start_up(origin)

            @pl.when(up == 0)
            def _():
                start_down(origin)

            rank_copy_in(origin).wait_recv()
            pack_and_send(origin, ranks[origin, 1])

        return carry

    def rank_copy_in(origin):
        return pltpu.make_async_remote_copy(
            src_ref=ranks.at[origin, 0],
            dst_ref=ranks.at[origin, 1],
            send_sem=rank_send.at[origin],
            recv_sem=rank_recv.at[origin],
            device_id=(dp, x * LAYER + origin * 2 + core),
            device_id_type=MESH,
        )

    lax.fori_loop(1, 2 * N_Z - 1, event, 0)

    left = lax.broadcasted_iota(jnp.int32, (half, 128), 1) < PANEL
    left_row = lax.broadcasted_iota(jnp.int32, (1, 128), 1) < PANEL

    def take_halves(ref, sweep):
        pieces = []
        for j in range(N_CENT // 2):
            even = ref[sweep, :, 256 * j : 256 * j + 128]
            odd = ref[sweep, :, 256 * j + 128 : 256 * j + 256]
            first_core = jnp.where(left_row, even, pltpu.roll(odd, 64, 1))
            second_core = jnp.where(left_row, pltpu.roll(even, 64, 1), odd)
            pieces.append(jnp.where(core == 0, first_core, second_core))
        return jnp.concatenate(pieces, axis=1)

    def split(row):
        high = row.astype(BF16).astype(F32)
        rest = row - high
        middle = rest.astype(BF16).astype(F32)
        last = rest - middle
        zeros = jnp.zeros((5, row.shape[1]), F32)
        return jnp.concatenate([high, middle, last, zeros], axis=0).astype(BF16)

    def pair_copy(source, target, sweep, i, send_sem, recv_sem):
        other = place_peer(i)
        return pltpu.make_async_remote_copy(
            src_ref=source.at[sweep, :, lanes((other // 2) * 128, 128)],
            dst_ref=target.at[sweep, :, lanes(here * 128, 128)],
            send_sem=send_sem.at[sweep],
            recv_sem=recv_sem.at[sweep],
            device_id=(dp, cent_of(other)),
            device_id_type=MESH,
        )

    def exchange_pairs(source, target, sweep, send_sem, recv_sem):
        def step(i, carry):
            pair_copy(source, target, sweep, i, send_sem, recv_sem).start()
            return carry

        lax.fori_loop(1, N_CENT, step, 0)
        target[sweep, :, lanes(here * 128, 128)] = source[sweep, :, lanes((here // 2) * 128, 128)]
        seen = target.at[sweep, :, pl.ds(0, (N_CENT - 1) * 128)]
        pltpu.make_async_copy(seen, seen, recv_sem.at[sweep]).wait()

    def edge_copy(sweep, i):
        return pltpu.make_async_remote_copy(
            src_ref=edge_out.at[sweep],
            dst_ref=edge_in.at[sweep, dp],
            send_sem=edge_send.at[sweep],
            recv_sem=edge_recv.at[sweep],
            device_id=(dp_peer(i), cent),
            device_id_type=MESH,
        )

    def panel_copy(sweep, target):
        return pltpu.make_async_remote_copy(
            src_ref=panel_out.at[sweep, target],
            dst_ref=panel_in.at[sweep, dp],
            send_sem=panel_send.at[sweep],
            recv_sem=panel_recv.at[sweep],
            device_id=(target, cent),
            device_id_type=MESH,
        )

    def sweep_step(sweep, carry):
        seen = fresh.at[sweep, pl.ds(0, N_DP - 1)]
        pltpu.make_async_copy(seen, seen, fresh_recv.at[sweep]).wait()
        top_squares = jnp.zeros((half, 128), F32)
        bottom_squares = jnp.zeros((half, 128), F32)
        for j in range(N_DP // 2):
            even = fresh[sweep, 2 * j].astype(F32)
            odd = fresh[sweep, 2 * j + 1].astype(F32)
            top = jnp.where(left, even, pltpu.roll(odd, 64, 1))
            bottom = jnp.where(left, pltpu.roll(even, 64, 1), odd)
            wide[:half, 128 * j : 128 * (j + 1)] = top
            wide[half:, 128 * j : 128 * (j + 1)] = bottom
            top_squares += top * top
            bottom_squares += bottom * bottom
        top_scale = lax.rsqrt(jnp.sum(top_squares, axis=1, keepdims=True) / D + EPSILON)
        bottom_scale = lax.rsqrt(jnp.sum(bottom_squares, axis=1, keepdims=True) / D + EPSILON)
        unit_cent[:half] = (wide[:half] * top_scale).astype(BF16)
        unit_cent[half:] = (wide[half:] * bottom_scale).astype(BF16)

        def score(g, inner):
            distance = (g + 1) // 2
            origin = z + jnp.where(lax.rem(g, 2) == 1, -distance, distance)

            @pl.when(jnp.logical_and(origin >= 0, origin < N_Z))
            def _():
                @pl.when(sweep == 0)
                def _():
                    def arrive(i, deep):
                        sender = lax.rem(x * 2 + core + i, LAYER)
                        slot = rows.at[origin * LAYER + sender]
                        pltpu.make_async_copy(
                            slot, slot, x_recv.at[origin * LAYER + sender]
                        ).wait()
                        return deep

                    lax.fori_loop(1, LAYER, arrive, 0)

                mine = rows[pl.ds(origin * LAYER, LAYER)].reshape(LAYER * CAP, D)
                scores = lax.dot_general(
                    unit_cent[...], mine, (((1,), (1,)), ((), ())), preferred_element_type=F32
                )
                weights = jnp.exp(scores * (SHARPNESS / D))
                raw[:, lanes(origin * LAYER * CAP, LAYER * CAP)] = weights
                part[sweep, :, lanes(origin * LAYER * CAP, LAYER * CAP)] = jnp.sum(
                    weights, axis=0, keepdims=True
                )

            return inner

        lax.fori_loop(0, 2 * N_Z - 1, score, 0)

        exchange_pairs(part, part_in, sweep, part_send, part_recv)
        parts = split(take_halves(part_in, sweep))
        sums_row = jnp.sum(
            jnp.dot(parts, own_pick[...], preferred_element_type=F32), axis=0, keepdims=True
        )
        total[sweep] = jnp.sum(
            lax.dot_general(
                split(sums_row),
                own_pick[...],
                (((1,), (1,)), ((), ())),
                preferred_element_type=F32,
            ),
            axis=0,
            keepdims=True,
        )
        exchange_pairs(total, total_in, sweep, total_send, total_recv)
        totals = take_halves(total_in, sweep)
        live = totals > 0.0
        inverse = jnp.where(live, 1.0 / jnp.where(live, totals, 1.0), 0.0)

        mass_part = jnp.zeros((BLOCK, 128), F32)
        for j in range(SLOTS // 128):
            piece = slice(128 * j, 128 * (j + 1))
            shares = raw[:, piece] * inverse[:, piece]
            low[:, piece] = shares.astype(BF16)
            mass_part += shares
        mass_row = jnp.sum(jnp.transpose(mass_part), axis=0, keepdims=True)
        edge_out[sweep, 2:3, :] = mass_row[:, :128]
        edge_out[sweep, 3:4, :] = mass_row[:, 128:]

        def sum_step(j, inner):
            block_rows = rows[:, :, lanes(j * 256, 256)].reshape(SLOTS, 256)
            sums = jnp.dot(low[...], block_rows, preferred_element_type=F32)
            for k in range(2):
                top = sums[:half, 128 * k : 128 * (k + 1)]
                bottom = sums[half:, 128 * k : 128 * (k + 1)]
                even = jnp.where(left, top, pltpu.roll(bottom, 64, 1))
                odd = jnp.where(left, pltpu.roll(top, 64, 1), bottom)
                panel_out[sweep, 4 * j + 2 * k] = even.astype(BF16)
                panel_out[sweep, 4 * j + 2 * k + 1] = odd.astype(BF16)
            for k in range(4):
                target = 4 * j + k

                @pl.when(target != dp)
                def _():
                    panel_copy(sweep, target).start()

            return inner

        lax.fori_loop(0, N_DP // 4, sum_step, 0)
        panel_in[sweep, dp] = panel_out[sweep, dp]
        seen = panel_in.at[sweep, pl.ds(0, N_DP - 1)]
        pltpu.make_async_copy(seen, seen, panel_recv.at[sweep]).wait()
        sums_panel = panel_in[sweep, 0].astype(F32)
        for j in range(1, N_DP):
            sums_panel += panel_in[sweep, j].astype(F32)

        squares = jnp.transpose(sums_panel * sums_panel)
        edge_out[sweep, 0:1, :] = jnp.sum(squares[:PANEL], axis=0, keepdims=True)
        edge_out[sweep, 1:2, :] = jnp.sum(squares[PANEL:], axis=0, keepdims=True)
        edge_out[sweep, 4:8, :] = jnp.zeros((4, 128), F32)

        def send_edge(i, inner):
            edge_copy(sweep, i).start()
            return inner

        lax.fori_loop(1, N_DP, send_edge, 0)
        edge_in[sweep, dp] = edge_out[sweep]
        seen = edge_in.at[sweep, pl.ds(0, N_DP - 1)]
        pltpu.make_async_copy(seen, seen, edge_recv.at[sweep]).wait()
        edges = edge_in[sweep, 0]
        for j in range(1, N_DP):
            edges += edge_in[sweep, j]
        scales = lax.rsqrt(edges / D + EPSILON)
        scale_t = jnp.concatenate(
            [
                jnp.broadcast_to(scales[0:1], (PANEL, 128)),
                jnp.broadcast_to(scales[1:2], (PANEL, 128)),
            ],
            axis=0,
        )
        new_panel = sums_panel * jnp.transpose(scale_t)

        @pl.when(sweep < ITERS - 1)
        def _():
            fresh[sweep + 1, dp] = new_panel.astype(BF16)
            send_fresh(sweep + 1)

        @pl.when(sweep == ITERS - 1)
        def _():
            out_ref[:half] = new_panel[:, :PANEL]
            out_ref[half:] = new_panel[:, PANEL:]
            mass_ref[:, :128] = edges[2:3]
            mass_ref[:, 128:] = edges[3:4]

        return carry

    lax.fori_loop(0, ITERS, sweep_step, 0)

    def leave(sweep, carry):
        for ref, sem in ((part_in, part_send), (total_in, total_send)):
            sent = ref.at[sweep, :, pl.ds(0, (N_CENT - 1) * 128)]
            pltpu.make_async_copy(sent, sent, sem.at[sweep]).wait()
        for ref, sem in ((panel_in, panel_send), (edge_in, edge_send), (fresh, fresh_send)):
            sent = ref.at[sweep, pl.ds(0, N_DP - 1)]
            pltpu.make_async_copy(sent, sent, sem.at[sweep]).wait()
        return carry

    lax.fori_loop(0, ITERS, leave, 0)

    def leave_origin(origin, carry):
        def step(i, inner):
            row_copy(origin, i).wait_send()
            return inner

        lax.fori_loop(1, LAYER, step, 0)

        @pl.when(jnp.logical_and(origin <= z, z < N_Z - 1))
        def _():
            unit_copy(origin, 1).wait_send()

        @pl.when(jnp.logical_and(origin >= z, z > 0))
        def _():
            unit_copy(origin, 0).wait_send()

        @pl.when(origin != z)
        def _():
            rank_copy(origin).wait_send()

        return carry

    lax.fori_loop(0, N_Z, leave_origin, 0)


def body(vectors, candidates, centroids):
    vmem = pl.BlockSpec(memory_space=pltpu.VMEM)
    dma = pltpu.SemaphoreType.DMA
    panel, mass = pl.pallas_call(
        kernel,
        out_shape=(
            jax.ShapeDtypeStruct((BLOCK, PANEL), F32),
            jax.ShapeDtypeStruct((1, BLOCK), F32),
        ),
        in_specs=[vmem] * 3,
        out_specs=(vmem, vmem),
        scratch_shapes=[
            pltpu.VMEM((N_Z, ROWS, D), BF16),
            pltpu.VMEM((N_Z, 2, LAYER, ROWS), jnp.int32),
            pltpu.VMEM((SLOTS, ROWS), BF16),
            pltpu.VMEM((N_Z, LAYER, CAP, D), BF16),
            pltpu.VMEM((N_CENT, CAP, D), BF16),
            pltpu.VMEM((BLOCK, SLOTS), F32),
            pltpu.VMEM((BLOCK, SLOTS), BF16),
            pltpu.VMEM((ITERS, 1, SLOTS), F32),
            pltpu.VMEM((ITERS, 1, N_CENT * 128), F32),
            pltpu.VMEM((ITERS, 1, SLOTS), F32),
            pltpu.VMEM((ITERS, 1, N_CENT * 128), F32),
            pltpu.VMEM((BLOCK, D), F32),
            pltpu.VMEM((BLOCK, D), BF16),
            pltpu.VMEM((ITERS, N_DP, 128, 128), BF16),
            pltpu.VMEM((ITERS, N_DP, 128, 128), BF16),
            pltpu.VMEM((ITERS, N_DP, 128, 128), BF16),
            pltpu.VMEM((ITERS, 8, 128), F32),
            pltpu.VMEM((ITERS, N_DP, 8, 128), F32),
            dma((N_Z, 2)),
            dma((N_Z,)),
            dma((N_Z,)),
            dma((N_Z,)),
            dma((N_Z, LAYER)),
            dma((N_CENT,)),
            dma((ITERS,)),
            dma((ITERS,)),
            dma((ITERS,)),
            dma((ITERS,)),
            dma((ITERS,)),
            dma((ITERS,)),
            dma((ITERS,)),
            dma((ITERS,)),
            dma((ITERS,)),
            dma((ITERS,)),
        ],
        compiler_params=pltpu.CompilerParams(
            collective_id=0, has_side_effects=True, vmem_limit_bytes=48 * 1024 * 1024
        ),
        cost_estimate=pl.CostEstimate(
            flops=9 * 2 * SLOTS * BLOCK * D // 2, bytes_accessed=4 << 20, transcendentals=SLOTS * BLOCK
        ),
        name="soft_kmeans",
    )(vectors, candidates.T, centroids)
    return panel, mass.reshape(BLOCK)


def solution(mesh):
    return jax.shard_map(
        body,
        mesh=mesh,
        in_specs=(P(("dp", "cent"), None), P(("dp", "cent"), None), P("cent", "dp")),
        out_specs=(P("cent", "dp"), P("cent")),
        check_vma=False,
    )
```

time: 859 us -> 177 us (0.21)
  the two profiles are of different devices: /device:TPU:2 before, /device:TPU:8 now
where the time goes in v1:
time: 177 us; the launch traced here: 176 us
  Pallas kernels  173 us (98%)
  local copies, waits for them, and re-layouts  3.19 us (2%)
    pallas_call x1, Pallas kernels, body(): pl.pallas_call(kernel, out_shape=(jax.ShapeDtypeStruct((BLOCK, PANEL), F3...  173 us

profile of v1, /device:TPU:8, one launch (start us, length us, event | category | flops | bytes accessed | tf_op | source)
XLA Modules:
  0.0 176.5 jit_solution(4224700280809177356)
XLA Ops:
  0.6 0.0 copy-start.1
  0.6 0.9 copy.5.cent_ref
  1.5 0.0 copy-done.1
  1.5 0.0 copy-start
  1.5 1.0 copy-done
  2.6 172.6 %soft_kmeans.1 = (f32[256,64]{1,0:T(8,128)S(1)}, f32[1,256]{1,0:T(1,128)S(1)}) custom-call(bf16[256,1024]{1,0:T(8,128)(2,1)S(1)} %copy-done, s32[4,256]{1,0:T(4,128)S(1)} %bitcast.3, bf16[256,64]{1,0:T(8,128)(2,1)S(1)} %copy.5.cent_ref), custom_call_target="tpu_custom_call" | custom-call | flops 4831838208 | bytes 4194304 | tf_op jit(solution)/shard_map/soft_kmeans/pallas_call | solution.py:510
  175.2 0.7 copy.6
  175.9 0.6 copy.8
Async XLA Ops:
  0.6 0.9 copy-start.1
  1.5 1.0 copy-start

commit v2 on v1

v2 whole, which is shorter than its diff:
```python
import functools

import jax
import jax.numpy as jnp
from jax import lax
from jax.experimental import pallas as pl
from jax.experimental.pallas import tpu as pltpu
from jax.sharding import PartitionSpec as P

ITERS = 2
EPSILON = 1e-06
SHARPNESS = 20.0

D = 1024
ROWS = 256
BLOCK = 256
CAP = 64
N_DP = 16
N_CENT = 32
N_X = 4
N_Y = 8
N_Z = 4
LAYER = 8
SLOTS = N_CENT * CAP
PANEL = D // N_DP

F32 = jnp.float32
BF16 = jnp.bfloat16
MESH = pl.DeviceIdType.MESH


def lanes(start, size):
    return pl.ds(pl.multiple_of(start, 128), size)


def kernel(
    vec_ref,
    cand_ref,
    cent_ref,
    out_ref,
    mass_ref,
    units,
    ranks,
    picks,
    packed,
    rows,
    raw,
    low,
    part,
    part_in,
    line_in,
    total,
    total_in,
    wide,
    unit_cent,
    panel_out,
    panel_in,
    fresh,
    edge_out,
    edge_in,
    z_send,
    z_recv,
    rank_send,
    rank_recv,
    x_send,
    x_recv,
    pair_sems,
    first_sems,
    part_send,
    part_recv,
    line_send,
    line_recv,
    total_send,
    total_recv,
    panel_send,
    panel_recv,
    fresh_send,
    fresh_recv,
    edge_send,
    edge_recv,
):
    dp = lax.axis_index("dp")
    cent = lax.axis_index("cent")
    x = cent // LAYER
    z = (cent // 2) % N_Z
    core = cent % 2
    seat = x * 2 + core

    def dp_peer(i):
        return lax.rem(dp + i, N_DP)

    def seat_peer(i):
        return lax.rem(seat + i, LAYER)

    def z_peer(i):
        return lax.rem(z + i, N_Z)

    def at_seat(other):
        return (dp, (other // 2) * LAYER + z * 2 + other % 2)

    def at_layer(other):
        return (dp, x * LAYER + other * 2 + core)

    barrier = pltpu.get_barrier_semaphore()

    def greet_seat(i, carry):
        pl.semaphore_signal(barrier, inc=1, device_id=at_seat(seat_peer(i)), device_id_type=MESH)
        return carry

    def greet_layer(i, carry):
        pl.semaphore_signal(barrier, inc=1, device_id=at_layer(z_peer(i)), device_id_type=MESH)
        return carry

    def greet_dp(i, carry):
        pl.semaphore_signal(barrier, inc=1, device_id=(dp_peer(i), cent), device_id_type=MESH)
        return carry

    lax.fori_loop(1, LAYER, greet_seat, 0)
    lax.fori_loop(1, N_Z, greet_layer, 0)
    lax.fori_loop(1, N_DP, greet_dp, 0)

    vec = vec_ref[...].astype(F32)
    vec_scale = lax.rsqrt(jnp.mean(vec * vec, axis=1, keepdims=True) + EPSILON)
    units[z] = (vec * vec_scale).astype(BF16)
    cand = cand_ref[...]
    place = lax.broadcasted_iota(jnp.int32, (N_CENT, ROWS), 0)
    block = ((place >> 1) & (N_X - 1)) * LAYER + (place >> 3) * 2 + (place & 1)
    named = cand[0:1, :] == block
    for j in range(1, cand.shape[0]):
        named = jnp.logical_or(named, cand[j : j + 1, :] == block)
    named_f = jnp.where(named, 1.0, 0.0)
    first = lax.broadcasted_iota(jnp.int32, (ROWS, ROWS), 0)
    second = lax.broadcasted_iota(jnp.int32, (ROWS, ROWS), 1)
    before = jnp.where(first < second, 1.0, 0.0).astype(BF16)
    rank = jnp.dot(named_f.astype(BF16), before, preferred_element_type=F32)
    slots = jnp.where(named, rank, -1.0).astype(jnp.int32)
    for layer in range(N_Z):
        ranks[layer, 0] = slots[layer * LAYER : (layer + 1) * LAYER]

    slot_iota = lax.broadcasted_iota(jnp.int32, (CAP, ROWS), 0)

    def pick_rows(rank_rows):
        picks = [
            jnp.where(rank_rows[j : j + 1, :] == slot_iota, 1.0, 0.0).astype(BF16)
            for j in range(LAYER)
        ]
        return jnp.concatenate(picks, axis=0)

    panel0 = cent_ref[...]
    half = BLOCK // 2
    quarter = half // 2
    for h in range(2):
        fresh[0, h, dp] = jnp.concatenate(
            [panel0[half * h : half * h + quarter], panel0[half * h + quarter : half * (h + 1)]],
            axis=1,
        )

    pl.semaphore_wait(barrier, LAYER - 1 + N_Z - 1 + N_DP - 1)

    def rank_copy(layer):
        return pltpu.make_async_remote_copy(
            src_ref=ranks.at[layer, 0],
            dst_ref=ranks.at[z, 1],
            send_sem=rank_send.at[layer],
            recv_sem=rank_recv.at[z],
            device_id=at_layer(layer),
            device_id_type=MESH,
        )

    def unit_copy(origin, side):
        return pltpu.make_async_remote_copy(
            src_ref=units.at[origin],
            dst_ref=units.at[origin],
            send_sem=z_send.at[origin, side],
            recv_sem=z_recv.at[origin],
            device_id=at_layer(z + 2 * side - 1),
            device_id_type=MESH,
        )

    def start_up(origin):
        @pl.when(z < N_Z - 1)
        def _():
            unit_copy(origin, 1).start()

    def start_down(origin):
        @pl.when(z > 0)
        def _():
            unit_copy(origin, 0).start()

    start_up(z)
    start_down(z)

    def send_rank(i, carry):
        rank_copy(z_peer(i)).start()
        return carry

    lax.fori_loop(1, N_Z, send_rank, 0)

    other_dp = lax.rem(dp + N_DP // 2, N_DP)
    pair_copy = pltpu.make_async_remote_copy(
        src_ref=fresh.at[0, :, dp],
        dst_ref=fresh.at[0, :, dp],
        send_sem=pair_sems.at[0],
        recv_sem=pair_sems.at[1],
        device_id=(other_dp, cent),
        device_id_type=MESH,
    )
    pair_copy.start()

    def first_copy(which, i):
        y_peer = (dp // N_Y) * N_Y + lax.rem(dp + i, N_Y)
        return pltpu.make_async_remote_copy(
            src_ref=fresh.at[0, :, which],
            dst_ref=fresh.at[0, :, which],
            send_sem=first_sems.at[0],
            recv_sem=first_sems.at[1],
            device_id=(y_peer, cent),
            device_id_type=MESH,
        )

    def fresh_copy(sweep, h, i):
        return pltpu.make_async_remote_copy(
            src_ref=fresh.at[sweep, h, dp],
            dst_ref=fresh.at[sweep, h, dp],
            send_sem=fresh_send.at[h],
            recv_sem=fresh_recv.at[h],
            device_id=(dp_peer(i), cent),
            device_id_type=MESH,
        )

    def row_copy(origin, i):
        target = seat_peer(i)
        return pltpu.make_async_remote_copy(
            src_ref=packed.at[origin, target],
            dst_ref=rows.at[origin * LAYER + seat],
            send_sem=x_send.at[origin, target],
            recv_sem=x_recv.at[origin * LAYER + seat],
            device_id=at_seat(target),
            device_id_type=MESH,
        )

    def pack_and_send(origin, rank_rows):
        picks[origin] = pick_rows(rank_rows)
        chosen = jnp.dot(picks[origin], units[origin], preferred_element_type=F32)
        packed[origin] = chosen.astype(BF16).reshape(LAYER, CAP, D)
        rows[origin * LAYER + seat] = packed[origin, seat]

        def step(i, carry):
            row_copy(origin, i).start()
            return carry

        lax.fori_loop(1, LAYER, step, 0)

    pack_and_send(z, ranks[z, 0])

    pair_copy.wait_recv()

    def send_first(i, carry):
        first_copy(dp, i).start()
        first_copy(other_dp, i).start()
        return carry

    lax.fori_loop(1, N_Y, send_first, 0)

    def event(e, carry):
        distance = (e + 1) // 2
        up = lax.rem(e, 2)
        origin = z + jnp.where(up == 1, -distance, distance)

        @pl.when(jnp.logical_and(origin >= 0, origin < N_Z))
        def _():
            unit_copy(origin, 0).wait_recv()

            @pl.when(up == 1)
            def _():
                start_up(origin)

            @pl.when(up == 0)
            def _():
                start_down(origin)

            rank_copy_in(origin).wait_recv()
            pack_and_send(origin, ranks[origin, 1])

        return carry

    def rank_copy_in(origin):
        return pltpu.make_async_remote_copy(
            src_ref=ranks.at[origin, 0],
            dst_ref=ranks.at[origin, 1],
            send_sem=rank_send.at[origin],
            recv_sem=rank_recv.at[origin],
            device_id=at_layer(origin),
            device_id_type=MESH,
        )

    lax.fori_loop(1, 2 * N_Z - 1, event, 0)

    left = lax.broadcasted_iota(jnp.int32, (quarter, 128), 1) < PANEL
    left_four = lax.broadcasted_iota(jnp.int32, (N_Z, 128), 1) < CAP
    left_row = lax.broadcasted_iota(jnp.int32, (1, 128), 1) < PANEL
    layer_iota = lax.broadcasted_iota(jnp.int32, (LAYER, 1), 0)

    def take_halves(ref, sweep):
        pieces = []
        for j in range(LAYER // 2):
            even = ref[sweep, 2 * j]
            odd = ref[sweep, 2 * j + 1]
            first_core = jnp.where(left_four, even, pltpu.roll(odd, 64, 1))
            second_core = jnp.where(left_four, pltpu.roll(even, 64, 1), odd)
            pieces.append(jnp.where(core == 0, first_core, second_core))
        return jnp.concatenate(pieces, axis=1)

    def split(four):
        zeros = jnp.zeros((LAYER - N_Z, four.shape[1]), F32)
        value = jnp.concatenate([four, zeros], axis=0)
        high = value.astype(BF16).astype(F32)
        rest = value - high
        middle = rest.astype(BF16).astype(F32)
        return jnp.concatenate([high, middle, rest - middle], axis=0).astype(BF16)

    def own_row(product, layer):
        added = product[:LAYER] + product[LAYER : 2 * LAYER] + product[2 * LAYER :]
        return jnp.where(layer_iota == layer, added, 0.0)

    def seat_copy(source, target, sweep, i, send_sem, recv_sem):
        other = seat_peer(i)
        return pltpu.make_async_remote_copy(
            src_ref=source.at[sweep, other // 2],
            dst_ref=target.at[sweep, seat],
            send_sem=send_sem.at[sweep],
            recv_sem=recv_sem.at[sweep],
            device_id=at_seat(other),
            device_id_type=MESH,
        )

    def exchange_seats(source, target, sweep, send_sem, recv_sem):
        def step(i, carry):
            seat_copy(source, target, sweep, i, send_sem, recv_sem).start()
            return carry

        lax.fori_loop(1, LAYER, step, 0)
        target[sweep, seat] = source[sweep, x]
        seen = target.at[sweep, pl.ds(0, LAYER - 1)]
        pltpu.make_async_copy(seen, seen, recv_sem.at[sweep]).wait()

    def line_copy(sweep, i):
        return pltpu.make_async_remote_copy(
            src_ref=line_in.at[sweep, z],
            dst_ref=line_in.at[sweep, z],
            send_sem=line_send.at[sweep],
            recv_sem=line_recv.at[sweep],
            device_id=at_layer(z_peer(i)),
            device_id_type=MESH,
        )

    def edge_copy(sweep, h, i):
        return pltpu.make_async_remote_copy(
            src_ref=edge_out.at[sweep, h],
            dst_ref=edge_in.at[sweep, h, dp],
            send_sem=edge_send.at[sweep, h],
            recv_sem=edge_recv.at[sweep, h],
            device_id=(dp_peer(i), cent),
            device_id_type=MESH,
        )

    def panel_copy(sweep, h, target):
        return pltpu.make_async_remote_copy(
            src_ref=panel_out.at[sweep, h, target],
            dst_ref=panel_in.at[sweep, h, dp],
            send_sem=panel_send.at[sweep, h],
            recv_sem=panel_recv.at[sweep, h],
            device_id=(target, cent),
            device_id_type=MESH,
        )

    def sweep_step(sweep, carry):
        @pl.when(sweep == 0)
        def _():
            seen = fresh.at[0, :, pl.ds(0, 2 * (N_Y - 1))]
            pltpu.make_async_copy(seen, seen, first_sems.at[1]).wait()

        for h in range(2):
            @pl.when(sweep > 0)
            def _():
                seen = fresh.at[sweep, h, pl.ds(0, N_DP - 1)]
                pltpu.make_async_copy(seen, seen, fresh_recv.at[h]).wait()

            low_row, high_row = half * h, half * h + quarter
            top_squares = jnp.zeros((quarter, 128), F32)
            bottom_squares = jnp.zeros((quarter, 128), F32)
            for j in range(N_DP // 2):
                even = fresh[sweep, h, 2 * j].astype(F32)
                odd = fresh[sweep, h, 2 * j + 1].astype(F32)
                top = jnp.where(left, even, pltpu.roll(odd, 64, 1))
                bottom = jnp.where(left, pltpu.roll(even, 64, 1), odd)
                wide[:quarter, 128 * j : 128 * (j + 1)] = top
                wide[quarter:, 128 * j : 128 * (j + 1)] = bottom
                top_squares += top * top
                bottom_squares += bottom * bottom
            top_scale = lax.rsqrt(jnp.sum(top_squares, axis=1, keepdims=True) / D + EPSILON)
            bottom_scale = lax.rsqrt(jnp.sum(bottom_squares, axis=1, keepdims=True) / D + EPSILON)
            unit_cent[low_row:high_row] = (wide[:quarter] * top_scale).astype(BF16)
            unit_cent[high_row : half * (h + 1)] = (wide[quarter:] * bottom_scale).astype(BF16)

        def score(g, inner):
            distance = (g + 1) // 2
            origin = z + jnp.where(lax.rem(g, 2) == 1, -distance, distance)

            @pl.when(jnp.logical_and(origin >= 0, origin < N_Z))
            def _():
                @pl.when(sweep == 0)
                def _():
                    def arrive(i, deep):
                        sender = lax.rem(seat + i, LAYER)
                        slot = rows.at[origin * LAYER + sender]
                        pltpu.make_async_copy(
                            slot, slot, x_recv.at[origin * LAYER + sender]
                        ).wait()
                        return deep

                    lax.fori_loop(1, LAYER, arrive, 0)

                mine = rows[pl.ds(origin * LAYER, LAYER)].reshape(LAYER * CAP, D)
                scores = lax.dot_general(
                    unit_cent[...], mine, (((1,), (1,)), ((), ())), preferred_element_type=F32
                )
                weights = jnp.exp(scores * (SHARPNESS / D))
                raw[:, lanes(origin * LAYER * CAP, LAYER * CAP)] = weights
                added = jnp.sum(weights, axis=0, keepdims=True)
                for j in range(N_X):
                    part[sweep, j, pl.ds(origin, 1), :] = added[:, 128 * j : 128 * (j + 1)]

            return inner

        lax.fori_loop(0, 2 * N_Z - 1, score, 0)

        exchange_seats(part, part_in, sweep, part_send, part_recv)
        parts = split(take_halves(part_in, sweep))
        by_row = jnp.zeros((LAYER, ROWS), F32)
        for layer in range(N_Z):
            product = jnp.dot(parts, picks[layer], preferred_element_type=F32)
            by_row += own_row(product, layer)
        line_in[sweep, z] = by_row[:N_Z]

        def send_line(i, inner):
            line_copy(sweep, i).start()
            return inner

        lax.fori_loop(1, N_Z, send_line, 0)
        seen = line_in.at[sweep, pl.ds(0, N_Z - 1)]
        pltpu.make_async_copy(seen, seen, line_recv.at[sweep]).wait()
        row_totals = line_in[sweep, 0]
        for layer in range(1, N_Z):
            row_totals += line_in[sweep, layer]
        parts = split(row_totals)
        by_slot = jnp.zeros((LAYER, LAYER * CAP), F32)
        for layer in range(N_Z):
            product = lax.dot_general(
                parts, picks[layer], (((1,), (1,)), ((), ())), preferred_element_type=F32
            )
            by_slot += own_row(product, layer)
        for j in range(N_X):
            total[sweep, j] = by_slot[:N_Z, 128 * j : 128 * (j + 1)]
        exchange_seats(total, total_in, sweep, total_send, total_recv)
        totals = take_halves(total_in, sweep)
        live = totals > 0.0
        inverse = jnp.where(live, 1.0 / jnp.where(live, totals, 1.0), 0.0)

        mass_part = jnp.zeros((BLOCK, 128), F32)
        for layer in range(N_Z):
            for j in range(N_X):
                start = layer * LAYER * CAP + 128 * j
                piece = slice(start, start + 128)
                shares = raw[:, piece] * inverse[layer : layer + 1, 128 * j : 128 * (j + 1)]
                low[:, piece] = shares.astype(BF16)
                mass_part += shares
        mass_row = jnp.sum(jnp.transpose(mass_part), axis=0, keepdims=True)
        for h in range(2):
            edge_out[sweep, h, 1:2, :] = mass_row[:, half * h : half * (h + 1)]

        def sum_step(i, inner):
            j = lax.rem(dp // 4 + i, N_DP // 4)
            block_rows = rows[:, :, lanes(j * 256, 256)].reshape(SLOTS, 256)
            sums = jnp.dot(low[...], block_rows, preferred_element_type=F32)
            for h in range(2):
                for k in range(2):
                    top = sums[half * h : half * h + quarter, 128 * k : 128 * (k + 1)]
                    bottom = sums[half * h + quarter : half * (h + 1), 128 * k : 128 * (k + 1)]
                    even = jnp.where(left, top, pltpu.roll(bottom, 64, 1))
                    odd = jnp.where(left, pltpu.roll(top, 64, 1), bottom)
                    panel_out[sweep, h, 4 * j + 2 * k] = even.astype(BF16)
                    panel_out[sweep, h, 4 * j + 2 * k + 1] = odd.astype(BF16)
            for k in range(4):
                target = 4 * j + lax.rem(dp + k, 4)

                @pl.when(target != dp)
                def _():
                    panel_copy(sweep, 0, target).start()

            return inner

        lax.fori_loop(0, N_DP // 4, sum_step, 0)

        def send_second(i, inner):
            panel_copy(sweep, 1, dp_peer(i)).start()
            return inner

        lax.fori_loop(1, N_DP, send_second, 0)

        for h in range(2):
            panel_in[sweep, h, dp] = panel_out[sweep, h, dp]
            seen = panel_in.at[sweep, h, pl.ds(0, N_DP - 1)]
            pltpu.make_async_copy(seen, seen, panel_recv.at[sweep, h]).wait()
            sums_panel = panel_in[sweep, h, 0].astype(F32)
            for j in range(1, N_DP):
                sums_panel += panel_in[sweep, h, j].astype(F32)

            squares = sums_panel * sums_panel
            squares = jnp.transpose(jnp.concatenate([squares, squares], axis=0))
            edge_out[sweep, h, 0:1, :] = jnp.where(
                left_row,
                jnp.sum(squares[:PANEL], axis=0, keepdims=True),
                jnp.sum(squares[PANEL:], axis=0, keepdims=True),
            )

            def send_edge(i, inner):
                edge_copy(sweep, h, i).start()
                return inner

            lax.fori_loop(1, N_DP, send_edge, 0)
            edge_in[sweep, h, dp] = edge_out[sweep, h]
            seen = edge_in.at[sweep, h, pl.ds(0, N_DP - 1)]
            pltpu.make_async_copy(seen, seen, edge_recv.at[sweep, h]).wait()
            edges = edge_in[sweep, h, 0]
            for j in range(1, N_DP):
                edges += edge_in[sweep, h, j]
            scales = lax.rsqrt(edges[0:1] / D + EPSILON)
            turned = pltpu.roll(scales, 64, 1)
            scale_t = jnp.concatenate(
                [
                    jnp.broadcast_to(jnp.where(left_row, scales, turned), (PANEL, 128)),
                    jnp.broadcast_to(jnp.where(left_row, turned, scales), (PANEL, 128)),
                ],
                axis=0,
            )
            new_panel = sums_panel * jnp.transpose(scale_t)[:quarter]

            @pl.when(sweep < ITERS - 1)
            def _():
                fresh[sweep + 1, h, dp] = new_panel.astype(BF16)

                def send_fresh(i, inner):
                    fresh_copy(sweep + 1, h, i).start()
                    return inner

                lax.fori_loop(1, N_DP, send_fresh, 0)

            @pl.when(sweep == ITERS - 1)
            def _():
                out_ref[half * h : half * h + quarter] = new_panel[:, :PANEL]
                out_ref[half * h + quarter : half * (h + 1)] = new_panel[:, PANEL:]
                mass_ref[:, half * h : half * (h + 1)] = edges[1:2]

        return carry

    lax.fori_loop(0, ITERS, sweep_step, 0)

    def leave(sweep, carry):
        for ref, sem, count in (
            (part_in, part_send, LAYER - 1),
            (line_in, line_send, N_Z - 1),
            (total_in, total_send, LAYER - 1),
        ):
            sent = ref.at[sweep, pl.ds(0, count)]
            pltpu.make_async_copy(sent, sent, sem.at[sweep]).wait()
        for h in range(2):
            for ref, sem in ((panel_in, panel_send), (edge_in, edge_send)):
                sent = ref.at[sweep, h, pl.ds(0, N_DP - 1)]
                pltpu.make_async_copy(sent, sent, sem.at[sweep, h]).wait()
        return carry

    lax.fori_loop(0, ITERS, leave, 0)
    for h in range(2):
        sent = fresh.at[1, h, pl.ds(0, N_DP - 1)]
        pltpu.make_async_copy(sent, sent, fresh_send.at[h]).wait()
    pair_copy.wait_send()
    sent = fresh.at[0, :, pl.ds(0, 2 * (N_Y - 1))]
    pltpu.make_async_copy(sent, sent, first_sems.at[0]).wait()

    def leave_origin(origin, carry):
        def step(i, inner):
            row_copy(origin, i).wait_send()
            return inner

        lax.fori_loop(1, LAYER, step, 0)

        @pl.when(jnp.logical_and(origin <= z, z < N_Z - 1))
        def _():
            unit_copy(origin, 1).wait_send()

        @pl.when(jnp.logical_and(origin >= z, z > 0))
        def _():
            unit_copy(origin, 0).wait_send()

        @pl.when(origin != z)
        def _():
            rank_copy(origin).wait_send()

        return carry

    lax.fori_loop(0, N_Z, leave_origin, 0)


def body(vectors, candidates, centroids):
    vmem = pl.BlockSpec(memory_space=pltpu.VMEM)
    dma = pltpu.SemaphoreType.DMA
    panel, mass = pl.pallas_call(
        kernel,
        out_shape=(
            jax.ShapeDtypeStruct((BLOCK, PANEL), F32),
            jax.ShapeDtypeStruct((1, BLOCK), F32),
        ),
        in_specs=[vmem] * 3,
        out_specs=(vmem, vmem),
        scratch_shapes=[
            pltpu.VMEM((N_Z, ROWS, D), BF16),
            pltpu.VMEM((N_Z, 2, LAYER, ROWS), jnp.int32),
            pltpu.VMEM((N_Z, LAYER * CAP, ROWS), BF16),
            pltpu.VMEM((N_Z, LAYER, CAP, D), BF16),
            pltpu.VMEM((N_CENT, CAP, D), BF16),
            pltpu.VMEM((BLOCK, SLOTS), F32),
            pltpu.VMEM((BLOCK, SLOTS), BF16),
            pltpu.VMEM((ITERS, N_X, N_Z, 128), F32),
            pltpu.VMEM((ITERS, LAYER, N_Z, 128), F32),
            pltpu.VMEM((ITERS, N_Z, N_Z, ROWS), F32),
            pltpu.VMEM((ITERS, N_X, N_Z, 128), F32),
            pltpu.VMEM((ITERS, LAYER, N_Z, 128), F32),
            pltpu.VMEM((BLOCK // 2, D), F32),
            pltpu.VMEM((BLOCK, D), BF16),
            pltpu.VMEM((ITERS, 2, N_DP, BLOCK // 4, 128), BF16),
            pltpu.VMEM((ITERS, 2, N_DP, BLOCK // 4, 128), BF16),
            pltpu.VMEM((ITERS, 2, N_DP, BLOCK // 4, 128), BF16),
            pltpu.VMEM((ITERS, 2, 2, 128), F32),
            pltpu.VMEM((ITERS, 2, N_DP, 2, 128), F32),
            dma((N_Z, 2)),
            dma((N_Z,)),
            dma((N_Z,)),
            dma((N_Z,)),
            dma((N_Z, LAYER)),
            dma((N_CENT,)),
            dma((2,)),
            dma((2,)),
            dma((ITERS,)),
            dma((ITERS,)),
            dma((ITERS,)),
            dma((ITERS,)),
            dma((ITERS,)),
            dma((ITERS,)),
            dma((ITERS, 2)),
            dma((ITERS, 2)),
            dma((2,)),
            dma((2,)),
            dma((ITERS, 2)),
            dma((ITERS, 2)),
        ],
        compiler_params=pltpu.CompilerParams(
            collective_id=0, has_side_effects=True, vmem_limit_bytes=48 * 1024 * 1024
        ),
        cost_estimate=pl.CostEstimate(
            flops=9 * 2 * SLOTS * BLOCK * D // 2, bytes_accessed=4 << 20, transcendentals=SLOTS * BLOCK
        ),
        name="soft_kmeans",
    )(vectors, candidates.T, centroids)
    return panel, mass.reshape(BLOCK)


def solution(mesh):
    return jax.shard_map(
        body,
        mesh=mesh,
        in_specs=(P(("dp", "cent"), None), P(("dp", "cent"), None), P("cent", "dp")),
        out_specs=(P("cent", "dp"), P("cent")),
        check_vma=False,
    )
```

time: 177 us -> 173 us (0.977)
  Pallas kernels: 173 us -> 168 us
    pallas_call x1, Pallas kernels: 173 us -> 168 us  [body(): pl.pallas_call(kernel, out_shape=(jax.ShapeDtypeStruct((BLOCK, PANEL), F3...]
where the time goes in v2:
time: 173 us; the launch traced here: 172 us
  Pallas kernels  168 us (97%)
  local copies, waits for them, and re-layouts  3.19 us (2%)
    pallas_call x1, Pallas kernels, body(): pl.pallas_call(kernel, out_shape=(jax.ShapeDtypeStruct((BLOCK, PANEL), F3...  168 us

profile of v2, /device:TPU:8, one launch (start us, length us, event | category | flops | bytes accessed | tf_op | source)
XLA Modules:
  0.0 172.3 jit_solution(16919791821968618863)
XLA Ops:
  0.6 0.0 copy-start.1
  0.6 0.9 copy.5.cent_ref
  1.5 0.0 copy-done.1
  1.5 0.0 copy-start
  1.5 1.0 copy-done
  2.6 168.4 %soft_kmeans.1 = (f32[256,64]{1,0:T(8,128)S(1)}, f32[1,256]{1,0:T(1,128)S(1)}) custom-call(bf16[256,1024]{1,0:T(8,128)(2,1)S(1)} %copy-done, s32[4,256]{1,0:T(4,128)S(1)} %bitcast.3, bf16[256,64]{1,0:T(8,128)(2,1)S(1)} %copy.5.cent_ref), custom_call_target="tpu_custom_call" | custom-call | flops 4831838208 | bytes 4194304 | tf_op jit(solution)/shard_map/soft_kmeans/pallas_call | solution.py:618
  171.0 0.7 copy.6
  171.7 0.6 copy.8
Async XLA Ops:
  0.6 0.9 copy-start.1
  1.5 1.0 copy-start

commit v3 on v2

--- a/solution.py
+++ b/solution.py
@@ -56,8 +56,10 @@
     panel_out,
     panel_in,
     fresh,
+    last_sums,
     edge_out,
     edge_in,
+    vouched,
     z_send,
     z_recv,
     rank_send,
@@ -89,6 +91,11 @@
     def dp_peer(i):
         return lax.rem(dp + i, N_DP)
 
+    def y_peer(i):
+        return (dp // N_Y) * N_Y + lax.rem(dp + i, N_Y)
+
+    other_dp = lax.rem(dp + N_Y, N_DP)
+
     def seat_peer(i):
         return lax.rem(seat + i, LAYER)
 
@@ -111,13 +118,14 @@
         pl.semaphore_signal(barrier, inc=1, device_id=at_layer(z_peer(i)), device_id_type=MESH)
         return carry
 
-    def greet_dp(i, carry):
-        pl.semaphore_signal(barrier, inc=1, device_id=(dp_peer(i), cent), device_id_type=MESH)
+    def greet_y(i, carry):
+        pl.semaphore_signal(barrier, inc=1, device_id=(y_peer(i), cent), device_id_type=MESH)
         return carry
 
     lax.fori_loop(1, LAYER, greet_seat, 0)
     lax.fori_loop(1, N_Z, greet_layer, 0)
-    lax.fori_loop(1, N_DP, greet_dp, 0)
+    lax.fori_loop(1, N_Y, greet_y, 0)
+    pl.semaphore_signal(barrier, inc=1, device_id=(other_dp, cent), device_id_type=MESH)
 
     vec = vec_ref[...].astype(F32)
     vec_scale = lax.rsqrt(jnp.mean(vec * vec, axis=1, keepdims=True) + EPSILON)
@@ -146,6 +154,12 @@
         ]
         return jnp.concatenate(picks, axis=0)
 
+    def pack(origin, rank_rows):
+        picks[origin] = pick_rows(rank_rows)
+        chosen = jnp.dot(picks[origin], units[origin], preferred_element_type=F32)
+        packed[origin] = chosen.astype(BF16).reshape(LAYER, CAP, D)
+        rows[origin * LAYER + seat] = packed[origin, seat]
+
     panel0 = cent_ref[...]
     half = BLOCK // 2
     quarter = half // 2
@@ -155,7 +169,10 @@
             axis=1,
         )
 
-    pl.semaphore_wait(barrier, LAYER - 1 + N_Z - 1 + N_DP - 1)
+    pack(z, ranks[z, 0])
+
+    pl.semaphore_wait(barrier, LAYER - 1 + N_Z - 1 + N_Y)
+    pl.semaphore_signal(vouched, inc=1, device_id=(other_dp, cent), device_id_type=MESH)
 
     def rank_copy(layer):
         return pltpu.make_async_remote_copy(
@@ -196,7 +213,6 @@
 
     lax.fori_loop(1, N_Z, send_rank, 0)
 
-    other_dp = lax.rem(dp + N_DP // 2, N_DP)
     pair_copy = pltpu.make_async_remote_copy(
         src_ref=fresh.at[0, :, dp],
         dst_ref=fresh.at[0, :, dp],
@@ -208,13 +224,12 @@
     pair_copy.start()
 
     def first_copy(which, i):
-        y_peer = (dp // N_Y) * N_Y + lax.rem(dp + i, N_Y)
         return pltpu.make_async_remote_copy(
             src_ref=fresh.at[0, :, which],
             dst_ref=fresh.at[0, :, which],
             send_sem=first_sems.at[0],
             recv_sem=first_sems.at[1],
-            device_id=(y_peer, cent),
+            device_id=(y_peer(i), cent),
             device_id_type=MESH,
         )
 
@@ -239,19 +254,14 @@
             device_id_type=MESH,
         )
 
-    def pack_and_send(origin, rank_rows):
-        picks[origin] = pick_rows(rank_rows)
-        chosen = jnp.dot(picks[origin], units[origin], preferred_element_type=F32)
-        packed[origin] = chosen.astype(BF16).reshape(LAYER, CAP, D)
-        rows[origin * LAYER + seat] = packed[origin, seat]
-
+    def send_packed(origin):
         def step(i, carry):
             row_copy(origin, i).start()
             return carry
 
         lax.fori_loop(1, LAYER, step, 0)
 
-    pack_and_send(z, ranks[z, 0])
+    send_packed(z)
 
     pair_copy.wait_recv()
 
@@ -280,7 +290,8 @@
                 start_down(origin)
 
             rank_copy_in(origin).wait_recv()
-            pack_and_send(origin, ranks[origin, 1])
+            pack(origin, ranks[origin, 1])
+            send_packed(origin)
 
         return carry
 
@@ -295,6 +306,7 @@
         )
 
     lax.fori_loop(1, 2 * N_Z - 1, event, 0)
+    pl.semaphore_wait(vouched, 1)
 
     left = lax.broadcasted_iota(jnp.int32, (quarter, 128), 1) < PANEL
     left_four = lax.broadcasted_iota(jnp.int32, (N_Z, 128), 1) < CAP
@@ -354,12 +366,12 @@
             device_id_type=MESH,
         )
 
-    def edge_copy(sweep, h, i):
-        return pltpu.make_async_remote_copy(
-            src_ref=edge_out.at[sweep, h],
-            dst_ref=edge_in.at[sweep, h, dp],
-            send_sem=edge_send.at[sweep, h],
-            recv_sem=edge_recv.at[sweep, h],
+    def edge_copy(h, i):
+        return pltpu.make_async_remote_copy(
+            src_ref=edge_out.at[h],
+            dst_ref=edge_in.at[h, dp],
+            send_sem=edge_send.at[h],
+            recv_sem=edge_recv.at[h],
             device_id=(dp_peer(i), cent),
             device_id_type=MESH,
         )
@@ -373,6 +385,11 @@
             device_id=(target, cent),
             device_id_type=MESH,
         )
+
+    def unit_scale(squares, sweep):
+        mean = jnp.sum(squares, axis=1, keepdims=True) / D
+        scale = jnp.where(sweep == 0, 1.0, lax.rsqrt(mean + EPSILON))
+        return scale * lax.rsqrt(mean * scale * scale + EPSILON)
 
     def sweep_step(sweep, carry):
         @pl.when(sweep == 0)
@@ -398,8 +415,8 @@
                 wide[quarter:, 128 * j : 128 * (j + 1)] = bottom
                 top_squares += top * top
                 bottom_squares += bottom * bottom
-            top_scale = lax.rsqrt(jnp.sum(top_squares, axis=1, keepdims=True) / D + EPSILON)
-            bottom_scale = lax.rsqrt(jnp.sum(bottom_squares, axis=1, keepdims=True) / D + EPSILON)
+            top_scale = unit_scale(top_squares, sweep)
+            bottom_scale = unit_scale(bottom_squares, sweep)
             unit_cent[low_row:high_row] = (wide[:quarter] * top_scale).astype(BF16)
             unit_cent[high_row : half * (h + 1)] = (wide[quarter:] * bottom_scale).astype(BF16)
 
@@ -477,7 +494,7 @@
                 mass_part += shares
         mass_row = jnp.sum(jnp.transpose(mass_part), axis=0, keepdims=True)
         for h in range(2):
-            edge_out[sweep, h, 1:2, :] = mass_row[:, half * h : half * (h + 1)]
+            edge_out[h, 1:2, :] = mass_row[:, half * h : half * (h + 1)]
 
         def sum_step(i, inner):
             j = lax.rem(dp // 4 + i, N_DP // 4)
@@ -516,39 +533,9 @@
             for j in range(1, N_DP):
                 sums_panel += panel_in[sweep, h, j].astype(F32)
 
-            squares = sums_panel * sums_panel
-            squares = jnp.transpose(jnp.concatenate([squares, squares], axis=0))
-            edge_out[sweep, h, 0:1, :] = jnp.where(
-                left_row,
-                jnp.sum(squares[:PANEL], axis=0, keepdims=True),
-                jnp.sum(squares[PANEL:], axis=0, keepdims=True),
-            )
-
-            def send_edge(i, inner):
-                edge_copy(sweep, h, i).start()
-                return inner
-
-            lax.fori_loop(1, N_DP, send_edge, 0)
-            edge_in[sweep, h, dp] = edge_out[sweep, h]
-            seen = edge_in.at[sweep, h, pl.ds(0, N_DP - 1)]
-            pltpu.make_async_copy(seen, seen, edge_recv.at[sweep, h]).wait()
-            edges = edge_in[sweep, h, 0]
-            for j in range(1, N_DP):
-                edges += edge_in[sweep, h, j]
-            scales = lax.rsqrt(edges[0:1] / D + EPSILON)
-            turned = pltpu.roll(scales, 64, 1)
-            scale_t = jnp.concatenate(
-                [
-                    jnp.broadcast_to(jnp.where(left_row, scales, turned), (PANEL, 128)),
-                    jnp.broadcast_to(jnp.where(left_row, turned, scales), (PANEL, 128)),
-                ],
-                axis=0,
-            )
-            new_panel = sums_panel * jnp.transpose(scale_t)[:quarter]
-
             @pl.when(sweep < ITERS - 1)
             def _():
-                fresh[sweep + 1, h, dp] = new_panel.astype(BF16)
+                fresh[sweep + 1, h, dp] = sums_panel.astype(BF16)
 
                 def send_fresh(i, inner):
                     fresh_copy(sweep + 1, h, i).start()
@@ -558,13 +545,45 @@
 
             @pl.when(sweep == ITERS - 1)
             def _():
-                out_ref[half * h : half * h + quarter] = new_panel[:, :PANEL]
-                out_ref[half * h + quarter : half * (h + 1)] = new_panel[:, PANEL:]
-                mass_ref[:, half * h : half * (h + 1)] = edges[1:2]
+                last_sums[h] = sums_panel
+                squares = sums_panel * sums_panel
+                squares = jnp.transpose(jnp.concatenate([squares, squares], axis=0))
+                edge_out[h, 0:1, :] = jnp.where(
+                    left_row,
+                    jnp.sum(squares[:PANEL], axis=0, keepdims=True),
+                    jnp.sum(squares[PANEL:], axis=0, keepdims=True),
+                )
+
+                def send_edge(i, inner):
+                    edge_copy(h, i).start()
+                    return inner
+
+                lax.fori_loop(1, N_DP, send_edge, 0)
+                edge_in[h, dp] = edge_out[h]
 
         return carry
 
     lax.fori_loop(0, ITERS, sweep_step, 0)
+
+    for h in range(2):
+        seen = edge_in.at[h, pl.ds(0, N_DP - 1)]
+        pltpu.make_async_copy(seen, seen, edge_recv.at[h]).wait()
+        edges = edge_in[h, 0]
+        for j in range(1, N_DP):
+            edges += edge_in[h, j]
+        scales = lax.rsqrt(edges[0:1] / D + EPSILON)
+        turned = pltpu.roll(scales, 64, 1)
+        scale_t = jnp.concatenate(
+            [
+                jnp.broadcast_to(jnp.where(left_row, scales, turned), (PANEL, 128)),
+                jnp.broadcast_to(jnp.where(left_row, turned, scales), (PANEL, 128)),
+            ],
+            axis=0,
+        )
+        new_panel = last_sums[h] * jnp.transpose(scale_t)[:quarter]
+        out_ref[half * h : half * h + quarter] = new_panel[:, :PANEL]
+        out_ref[half * h + quarter : half * (h + 1)] = new_panel[:, PANEL:]
+        mass_ref[:, half * h : half * (h + 1)] = edges[1:2]
 
     def leave(sweep, carry):
         for ref, sem, count in (
@@ -575,15 +594,16 @@
             sent = ref.at[sweep, pl.ds(0, count)]
             pltpu.make_async_copy(sent, sent, sem.at[sweep]).wait()
         for h in range(2):
-            for ref, sem in ((panel_in, panel_send), (edge_in, edge_send)):
-                sent = ref.at[sweep, h, pl.ds(0, N_DP - 1)]
-                pltpu.make_async_copy(sent, sent, sem.at[sweep, h]).wait()
+            sent = panel_in.at[sweep, h, pl.ds(0, N_DP - 1)]
+            pltpu.make_async_copy(sent, sent, panel_send.at[sweep, h]).wait()
         return carry
 
     lax.fori_loop(0, ITERS, leave, 0)
     for h in range(2):
         sent = fresh.at[1, h, pl.ds(0, N_DP - 1)]
         pltpu.make_async_copy(sent, sent, fresh_send.at[h]).wait()
+        sent = edge_in.at[h, pl.ds(0, N_DP - 1)]
+        pltpu.make_async_copy(sent, sent, edge_send.at[h]).wait()
     pair_copy.wait_send()
     sent = fresh.at[0, :, pl.ds(0, 2 * (N_Y - 1))]
     pltpu.make_async_copy(sent, sent, first_sems.at[0]).wait()
@@ -641,8 +661,10 @@
             pltpu.VMEM((ITERS, 2, N_DP, BLOCK // 4, 128), BF16),
             pltpu.VMEM((ITERS, 2, N_DP, BLOCK // 4, 128), BF16),
             pltpu.VMEM((ITERS, 2, N_DP, BLOCK // 4, 128), BF16),
-            pltpu.VMEM((ITERS, 2, 2, 128), F32),
-            pltpu.VMEM((ITERS, 2, N_DP, 2, 128), F32),
+            pltpu.VMEM((2, BLOCK // 4, 128), F32),
+            pltpu.VMEM((2, 2, 128), F32),
+            pltpu.VMEM((2, N_DP, 2, 128), F32),
+            pltpu.SemaphoreType.REGULAR,
             dma((N_Z, 2)),
             dma((N_Z,)),
             dma((N_Z,)),
@@ -661,8 +683,8 @@
             dma((ITERS, 2)),
             dma((2,)),
             dma((2,)),
-            dma((ITERS, 2)),
-            dma((ITERS, 2)),
+            dma((2,)),
+            dma((2,)),
         ],
         compiler_params=pltpu.CompilerParams(
             collective_id=0, has_side_effects=True, vmem_limit_bytes=48 * 1024 * 1024

time: 173 us -> 155 us (0.90)
  Pallas kernels: 168 us -> 151 us
    pallas_call x1, Pallas kernels: 168 us -> 151 us  [body(): pl.pallas_call(kernel, out_shape=(jax.ShapeDtypeStruct((BLOCK, PANEL), F3...]
where the time goes in v3:
time: 155 us
  Pallas kernels  151 us (97%)
  local copies, waits for them, and re-layouts  3.19 us (2%)
    pallas_call x1, Pallas kernels, body(): pl.pallas_call(kernel, out_shape=(jax.ShapeDtypeStruct((BLOCK, PANEL), F3...  151 us
    unnamed x7, local copies, waits for them, and re-layouts  3.19 us

profile of v3, /device:TPU:8, one launch (start us, length us, event | category | flops | bytes accessed | tf_op | source)
XLA Modules:
  0.0 155.1 jit_solution(4352450193838298133)
XLA Ops:
  0.6 0.0 copy-start.1
  0.6 0.9 copy.5.cent_ref
  1.5 0.0 copy-done.1
  1.5 0.0 copy-start
  1.5 1.0 copy-done
  2.6 151.2 %soft_kmeans.1 = (f32[256,64]{1,0:T(8,128)S(1)}, f32[1,256]{1,0:T(1,128)S(1)}) custom-call(bf16[256,1024]{1,0:T(8,128)(2,1)S(1)} %copy-done, s32[4,256]{1,0:T(4,128)S(1)} %bitcast.3, bf16[256,64]{1,0:T(8,128)(2,1)S(1)} %copy.5.cent_ref), custom_call_target="tpu_custom_call" | custom-call | flops 4831838208 | bytes 4194304 | tf_op jit(solution)/shard_map/soft_kmeans/pallas_call | solution.py:638
  153.8 0.7 copy.6
  154.5 0.6 copy.8
Async XLA Ops:
  0.6 0.9 copy-start.1
  1.5 1.0 copy-start

commit v4 on v3

--- a/solution.py
+++ b/solution.py
@@ -34,11 +34,15 @@
 
 
 def kernel(
+    vec_hbm,
+    cand_hbm,
+    cent_hbm,
+    out_ref,
+    mass_ref,
     vec_ref,
     cand_ref,
     cent_ref,
-    out_ref,
-    mass_ref,
+    fetch_sems,
     units,
     ranks,
     picks,
@@ -88,16 +92,20 @@
     core = cent % 2
     seat = x * 2 + core
 
+    def offset(i):
+        return 4 + i // 2 - lax.rem(i, 2) * (2 * (i // 2) + 1)
+
     def dp_peer(i):
-        return lax.rem(dp + i, N_DP)
+        z_of = lax.rem(dp // N_Y + 1 - lax.rem(i, 2), 2)
+        return z_of * N_Y + lax.rem(dp + offset(i // 2), N_Y)
 
     def y_peer(i):
-        return (dp // N_Y) * N_Y + lax.rem(dp + i, N_Y)
+        return (dp // N_Y) * N_Y + lax.rem(dp + offset(i), N_Y)
 
     other_dp = lax.rem(dp + N_Y, N_DP)
 
     def seat_peer(i):
-        return lax.rem(seat + i, LAYER)
+        return lax.rem(seat + offset(i), LAYER)
 
     def z_peer(i):
         return lax.rem(z + i, N_Z)
@@ -122,10 +130,23 @@
         pl.semaphore_signal(barrier, inc=1, device_id=(y_peer(i), cent), device_id_type=MESH)
         return carry
 
-    lax.fori_loop(1, LAYER, greet_seat, 0)
+    lax.fori_loop(0, LAYER - 1, greet_seat, 0)
     lax.fori_loop(1, N_Z, greet_layer, 0)
-    lax.fori_loop(1, N_Y, greet_y, 0)
+    lax.fori_loop(0, N_Y - 1, greet_y, 0)
     pl.semaphore_signal(barrier, inc=1, device_id=(other_dp, cent), device_id_type=MESH)
+
+    fetches = [
+        pltpu.make_async_copy(source, place, sem)
+        for source, place, sem in (
+            (vec_hbm, vec_ref, fetch_sems.at[0]),
+            (cand_hbm, cand_ref, fetch_sems.at[1]),
+            (cent_hbm, cent_ref, fetch_sems.at[2]),
+        )
+    ]
+    for fetch in fetches:
+        fetch.start()
+    for fetch in fetches:
+        fetch.wait()
 
     vec = vec_ref[...].astype(F32)
     vec_scale = lax.rsqrt(jnp.mean(vec * vec, axis=1, keepdims=True) + EPSILON)
@@ -160,58 +181,18 @@
         packed[origin] = chosen.astype(BF16).reshape(LAYER, CAP, D)
         rows[origin * LAYER + seat] = packed[origin, seat]
 
-    panel0 = cent_ref[...]
     half = BLOCK // 2
     quarter = half // 2
+    left = lax.broadcasted_iota(jnp.int32, (quarter, 128), 1) < PANEL
     for h in range(2):
-        fresh[0, h, dp] = jnp.concatenate(
-            [panel0[half * h : half * h + quarter], panel0[half * h + quarter : half * (h + 1)]],
-            axis=1,
-        )
+        across = cent_ref[:, half * h : half * (h + 1)].astype(F32)
+        along = jnp.transpose(jnp.concatenate([across, across], axis=0))
+        fresh[0, h, dp] = jnp.where(left, along[:quarter], along[quarter:]).astype(BF16)
 
     pack(z, ranks[z, 0])
 
     pl.semaphore_wait(barrier, LAYER - 1 + N_Z - 1 + N_Y)
     pl.semaphore_signal(vouched, inc=1, device_id=(other_dp, cent), device_id_type=MESH)
-
-    def rank_copy(layer):
-        return pltpu.make_async_remote_copy(
-            src_ref=ranks.at[layer, 0],
-            dst_ref=ranks.at[z, 1],
-            send_sem=rank_send.at[layer],
-            recv_sem=rank_recv.at[z],
-            device_id=at_layer(layer),
-            device_id_type=MESH,
-        )
-
-    def unit_copy(origin, side):
-        return pltpu.make_async_remote_copy(
-            src_ref=units.at[origin],
-            dst_ref=units.at[origin],
-            send_sem=z_send.at[origin, side],
-            recv_sem=z_recv.at[origin],
-            device_id=at_layer(z + 2 * side - 1),
-            device_id_type=MESH,
-        )
-
-    def start_up(origin):
-        @pl.when(z < N_Z - 1)
-        def _():
-            unit_copy(origin, 1).start()
-
-    def start_down(origin):
-        @pl.when(z > 0)
-        def _():
-            unit_copy(origin, 0).start()
-
-    start_up(z)
-    start_down(z)
-
-    def send_rank(i, carry):
-        rank_copy(z_peer(i)).start()
-        return carry
-
-    lax.fori_loop(1, N_Z, send_rank, 0)
 
     pair_copy = pltpu.make_async_remote_copy(
         src_ref=fresh.at[0, :, dp],
@@ -223,6 +204,46 @@
     )
     pair_copy.start()
 
+    def rank_copy(layer):
+        return pltpu.make_async_remote_copy(
+            src_ref=ranks.at[layer, 0],
+            dst_ref=ranks.at[z, 1],
+            send_sem=rank_send.at[layer],
+            recv_sem=rank_recv.at[z],
+            device_id=at_layer(layer),
+            device_id_type=MESH,
+        )
+
+    def unit_copy(origin, side):
+        return pltpu.make_async_remote_copy(
+            src_ref=units.at[origin],
+            dst_ref=units.at[origin],
+            send_sem=z_send.at[origin, side],
+            recv_sem=z_recv.at[origin],
+            device_id=at_layer(z + 2 * side - 1),
+            device_id_type=MESH,
+        )
+
+    def start_up(origin):
+        @pl.when(z < N_Z - 1)
+        def _():
+            unit_copy(origin, 1).start()
+
+    def start_down(origin):
+        @pl.when(z > 0)
+        def _():
+            unit_copy(origin, 0).start()
+
+    start_up(z)
+    start_down(z)
+
+    def send_rank(i, carry):
+        rank_copy(z_peer(i)).start()
+        return carry
+
+    lax.fori_loop(1, N_Z, send_rank, 0)
+
+
     def first_copy(which, i):
         return pltpu.make_async_remote_copy(
             src_ref=fresh.at[0, :, which],
@@ -259,18 +280,9 @@
             row_copy(origin, i).start()
             return carry
 
-        lax.fori_loop(1, LAYER, step, 0)
+        lax.fori_loop(0, LAYER - 1, step, 0)
 
     send_packed(z)
-
-    pair_copy.wait_recv()
-
-    def send_first(i, carry):
-        first_copy(dp, i).start()
-        first_copy(other_dp, i).start()
-        return carry
-
-    lax.fori_loop(1, N_Y, send_first, 0)
 
     def event(e, carry):
         distance = (e + 1) // 2
@@ -305,12 +317,19 @@
             device_id_type=MESH,
         )
 
-    lax.fori_loop(1, 2 * N_Z - 1, event, 0)
+    lax.fori_loop(1, 3, event, 0)
+    pair_copy.wait_recv()
+
+    def send_first(i, carry):
+        first_copy(dp, i).start()
+        first_copy(other_dp, i).start()
+        return carry
+
+    lax.fori_loop(0, N_Y - 1, send_first, 0)
+    lax.fori_loop(3, 2 * N_Z - 1, event, 0)
     pl.semaphore_wait(vouched, 1)
 
-    left = lax.broadcasted_iota(jnp.int32, (quarter, 128), 1) < PANEL
     left_four = lax.broadcasted_iota(jnp.int32, (N_Z, 128), 1) < CAP
-    left_row = lax.broadcasted_iota(jnp.int32, (1, 128), 1) < PANEL
     layer_iota = lax.broadcasted_iota(jnp.int32, (LAYER, 1), 0)
 
     def take_halves(ref, sweep):
@@ -351,7 +370,7 @@
             seat_copy(source, target, sweep, i, send_sem, recv_sem).start()
             return carry
 
-        lax.fori_loop(1, LAYER, step, 0)
+        lax.fori_loop(0, LAYER - 1, step, 0)
         target[sweep, seat] = source[sweep, x]
         seen = target.at[sweep, pl.ds(0, LAYER - 1)]
         pltpu.make_async_copy(seen, seen, recv_sem.at[sweep]).wait()
@@ -392,17 +411,7 @@
         return scale * lax.rsqrt(mean * scale * scale + EPSILON)
 
     def sweep_step(sweep, carry):
-        @pl.when(sweep == 0)
-        def _():
-            seen = fresh.at[0, :, pl.ds(0, 2 * (N_Y - 1))]
-            pltpu.make_async_copy(seen, seen, first_sems.at[1]).wait()
-
-        for h in range(2):
-            @pl.when(sweep > 0)
-            def _():
-                seen = fresh.at[sweep, h, pl.ds(0, N_DP - 1)]
-                pltpu.make_async_copy(seen, seen, fresh_recv.at[h]).wait()
-
+        def unit_half(h):
             low_row, high_row = half * h, half * h + quarter
             top_squares = jnp.zeros((quarter, 128), F32)
             bottom_squares = jnp.zeros((quarter, 128), F32)
@@ -420,37 +429,63 @@
             unit_cent[low_row:high_row] = (wide[:quarter] * top_scale).astype(BF16)
             unit_cent[high_row : half * (h + 1)] = (wide[quarter:] * bottom_scale).astype(BF16)
 
-        def score(g, inner):
-            distance = (g + 1) // 2
-            origin = z + jnp.where(lax.rem(g, 2) == 1, -distance, distance)
-
-            @pl.when(jnp.logical_and(origin >= 0, origin < N_Z))
-            def _():
-                @pl.when(sweep == 0)
+        def score(origin, start, size):
+            mine = rows[pl.ds(origin * LAYER, LAYER)].reshape(LAYER * CAP, D)
+            scores = lax.dot_general(
+                unit_cent[start : start + size],
+                mine,
+                (((1,), (1,)), ((), ())),
+                preferred_element_type=F32,
+            )
+            weights = jnp.exp(scores * (SHARPNESS / D))
+            raw[start : start + size, lanes(origin * LAYER * CAP, LAYER * CAP)] = weights
+            added = jnp.sum(weights, axis=0, keepdims=True)
+            for j in range(N_X):
+                piece = added[:, 128 * j : 128 * (j + 1)]
+                if start > 0:
+                    piece += part[sweep, j, pl.ds(origin, 1), :]
+                part[sweep, j, pl.ds(origin, 1), :] = piece
+
+        @pl.when(sweep == 0)
+        def _():
+            seen = fresh.at[0, :, pl.ds(0, 2 * (N_Y - 1))]
+            pltpu.make_async_copy(seen, seen, first_sems.at[1]).wait()
+            for h in range(2):
+                unit_half(h)
+
+            def score_arrived(g, inner):
+                distance = (g + 1) // 2
+                origin = z + jnp.where(lax.rem(g, 2) == 1, -distance, distance)
+
+                @pl.when(jnp.logical_and(origin >= 0, origin < N_Z))
                 def _():
                     def arrive(i, deep):
-                        sender = lax.rem(seat + i, LAYER)
+                        sender = seat_peer(i)
                         slot = rows.at[origin * LAYER + sender]
                         pltpu.make_async_copy(
                             slot, slot, x_recv.at[origin * LAYER + sender]
                         ).wait()
                         return deep
 
-                    lax.fori_loop(1, LAYER, arrive, 0)
-
-                mine = rows[pl.ds(origin * LAYER, LAYER)].reshape(LAYER * CAP, D)
-                scores = lax.dot_general(
-                    unit_cent[...], mine, (((1,), (1,)), ((), ())), preferred_element_type=F32
-                )
-                weights = jnp.exp(scores * (SHARPNESS / D))
-                raw[:, lanes(origin * LAYER * CAP, LAYER * CAP)] = weights
-                added = jnp.sum(weights, axis=0, keepdims=True)
-                for j in range(N_X):
-                    part[sweep, j, pl.ds(origin, 1), :] = added[:, 128 * j : 128 * (j + 1)]
-
-            return inner
-
-        lax.fori_loop(0, 2 * N_Z - 1, score, 0)
+                    lax.fori_loop(0, LAYER - 1, arrive, 0)
+                    score(origin, 0, BLOCK)
+
+                return inner
+
+            lax.fori_loop(0, 2 * N_Z - 1, score_arrived, 0)
+
+        @pl.when(sweep > 0)
+        def _():
+            for h in range(2):
+                seen = fresh.at[sweep, h, pl.ds(0, N_DP - 1)]
+                pltpu.make_async_copy(seen, seen, fresh_recv.at[h]).wait()
+                unit_half(h)
+
+                def score_half(origin, inner):
+                    score(origin, half * h, half)
+                    return inner
+
+                lax.fori_loop(0, N_Z, score_half, 0)
 
         exchange_seats(part, part_in, sweep, part_send, part_recv)
         parts = split(take_halves(part_in, sweep))
@@ -497,7 +532,9 @@
             edge_out[h, 1:2, :] = mass_row[:, half * h : half * (h + 1)]
 
         def sum_step(i, inner):
-            j = lax.rem(dp // 4 + i, N_DP // 4)
+            far_z = lax.rem(dp // N_Y + 1 - lax.rem(i, 2), 2)
+            far_y = lax.rem(dp // 4 + 1 - i // 2, 2)
+            j = far_z * 2 + far_y
             block_rows = rows[:, :, lanes(j * 256, 256)].reshape(SLOTS, 256)
             sums = jnp.dot(low[...], block_rows, preferred_element_type=F32)
             for h in range(2):
@@ -509,7 +546,7 @@
                     panel_out[sweep, h, 4 * j + 2 * k] = even.astype(BF16)
                     panel_out[sweep, h, 4 * j + 2 * k + 1] = odd.astype(BF16)
             for k in range(4):
-                target = 4 * j + lax.rem(dp + k, 4)
+                target = 4 * j + lax.rem(dp + 2 + k, 4)
 
                 @pl.when(target != dp)
                 def _():
@@ -523,7 +560,7 @@
             panel_copy(sweep, 1, dp_peer(i)).start()
             return inner
 
-        lax.fori_loop(1, N_DP, send_second, 0)
+        lax.fori_loop(0, N_DP - 1, send_second, 0)
 
         for h in range(2):
             panel_in[sweep, h, dp] = panel_out[sweep, h, dp]
@@ -541,24 +578,20 @@
                     fresh_copy(sweep + 1, h, i).start()
                     return inner
 
-                lax.fori_loop(1, N_DP, send_fresh, 0)
+                lax.fori_loop(0, N_DP - 1, send_fresh, 0)
 
             @pl.when(sweep == ITERS - 1)
             def _():
-                last_sums[h] = sums_panel
-                squares = sums_panel * sums_panel
-                squares = jnp.transpose(jnp.concatenate([squares, squares], axis=0))
-                edge_out[h, 0:1, :] = jnp.where(
-                    left_row,
-                    jnp.sum(squares[:PANEL], axis=0, keepdims=True),
-                    jnp.sum(squares[PANEL:], axis=0, keepdims=True),
-                )
+                along = jnp.transpose(jnp.concatenate([sums_panel, sums_panel], axis=0))
+                across = jnp.where(left, along[:PANEL], along[PANEL:])
+                last_sums[h] = across
+                edge_out[h, 0:1, :] = jnp.sum(across * across, axis=0, keepdims=True)
 
                 def send_edge(i, inner):
                     edge_copy(h, i).start()
                     return inner
 
-                lax.fori_loop(1, N_DP, send_edge, 0)
+                lax.fori_loop(0, N_DP - 1, send_edge, 0)
                 edge_in[h, dp] = edge_out[h]
 
         return carry
@@ -572,17 +605,7 @@
         for j in range(1, N_DP):
             edges += edge_in[h, j]
         scales = lax.rsqrt(edges[0:1] / D + EPSILON)
-        turned = pltpu.roll(scales, 64, 1)
-        scale_t = jnp.concatenate(
-            [
-                jnp.broadcast_to(jnp.where(left_row, scales, turned), (PANEL, 128)),
-                jnp.broadcast_to(jnp.where(left_row, turned, scales), (PANEL, 128)),
-            ],
-            axis=0,
-        )
-        new_panel = last_sums[h] * jnp.transpose(scale_t)[:quarter]
-        out_ref[half * h : half * h + quarter] = new_panel[:, :PANEL]
-        out_ref[half * h + quarter : half * (h + 1)] = new_panel[:, PANEL:]
+        out_ref[:, half * h : half * (h + 1)] = last_sums[h] * scales
         mass_ref[:, half * h : half * (h + 1)] = edges[1:2]
 
     def leave(sweep, carry):
@@ -613,7 +636,7 @@
             row_copy(origin, i).wait_send()
             return inner
 
-        lax.fori_loop(1, LAYER, step, 0)
+        lax.fori_loop(0, LAYER - 1, step, 0)
 
         @pl.when(jnp.logical_and(origin <= z, z < N_Z - 1))
         def _():
@@ -638,12 +661,16 @@
     panel, mass = pl.pallas_call(
         kernel,
         out_shape=(
-            jax.ShapeDtypeStruct((BLOCK, PANEL), F32),
+            jax.ShapeDtypeStruct((PANEL, BLOCK), F32),
             jax.ShapeDtypeStruct((1, BLOCK), F32),
         ),
-        in_specs=[vmem] * 3,
+        in_specs=[pl.BlockSpec(memory_space=pltpu.HBM)] * 3,
         out_specs=(vmem, vmem),
         scratch_shapes=[
+            pltpu.VMEM((ROWS, D), BF16),
+            pltpu.VMEM(candidates.shape[::-1], jnp.int32),
+            pltpu.VMEM((PANEL, BLOCK), BF16),
+            dma((3,)),
             pltpu.VMEM((N_Z, ROWS, D), BF16),
             pltpu.VMEM((N_Z, 2, LAYER, ROWS), jnp.int32),
             pltpu.VMEM((N_Z, LAYER * CAP, ROWS), BF16),
@@ -661,7 +688,7 @@
             pltpu.VMEM((ITERS, 2, N_DP, BLOCK // 4, 128), BF16),
             pltpu.VMEM((ITERS, 2, N_DP, BLOCK // 4, 128), BF16),
             pltpu.VMEM((ITERS, 2, N_DP, BLOCK // 4, 128), BF16),
-            pltpu.VMEM((2, BLOCK // 4, 128), F32),
+            pltpu.VMEM((2, PANEL, 128), F32),
             pltpu.VMEM((2, 2, 128), F32),
             pltpu.VMEM((2, N_DP, 2, 128), F32),
             pltpu.SemaphoreType.REGULAR,
@@ -687,14 +714,14 @@
             dma((2,)),
         ],
         compiler_params=pltpu.CompilerParams(
-            collective_id=0, has_side_effects=True, vmem_limit_bytes=48 * 1024 * 1024
+            collective_id=0, has_side_effects=True, vmem_limit_bytes=60 * 1024 * 1024
         ),
         cost_estimate=pl.CostEstimate(
             flops=9 * 2 * SLOTS * BLOCK * D // 2, bytes_accessed=4 << 20, transcendentals=SLOTS * BLOCK
         ),
         name="soft_kmeans",
-    )(vectors, candidates.T, centroids)
-    return panel, mass.reshape(BLOCK)
+    )(vectors, candidates.T, centroids.T)
+    return panel.T, mass.reshape(BLOCK)
 
 
 def solution(mesh):

time: 155 us -> 148 us (0.955)
  Pallas kernels: 151 us -> 145 us
    pallas_call x1, Pallas kernels: 151 us -> 145 us  [body(): pl.pallas_call(kernel, out_shape=(jax.ShapeDtypeStruct((PANEL, BLOCK), F3...]
    unnamed x7 -> x4, local copies, waits for them, and re-layouts: 3.19 us -> 2.04 us
where the time goes in v4:
time: 148 us
  Pallas kernels  145 us (98%)
  local copies, waits for them, and re-layouts  2.04 us (1%)
    pallas_call x1, Pallas kernels, body(): pl.pallas_call(kernel, out_shape=(jax.ShapeDtypeStruct((PANEL, BLOCK), F3...  145 us

profile of v4, /device:TPU:8, one launch (start us, length us, event | category | flops | bytes accessed | tf_op | source)
XLA Modules:
  0.0 147.8 jit_solution(8129435861164555594)
XLA Ops:
  0.6 145.1 %soft_kmeans.1 = (f32[64,256]{1,0:T(8,128)}, f32[1,256]{1,0:T(1,128)}) custom-call(bf16[256,1024]{1,0:T(8,128)(2,1)} %vec_hbm.1, s32[4,256]{1,0:T(4,128)} %bitcast.7, bf16[64,256]{1,0:T(8,128)(2,1)} %bitcast.6), custom_call_target="tpu_custom_call" | custom-call | flops 4831838208 | bytes 4194304 | tf_op jit(solution)/shard_map/soft_kmeans/pallas_call | solution.py:661
  145.8 0.0 copy-start
  145.8 1.5 copy.7
  147.3 0.0 copy-done
  147.3 0.6 copy.8
Async XLA Ops:
  145.8 1.5 %copy-start = (f32[1,256]{1,0:T(1,128)S(1)}, f32[1,256]{1,0:T(1,128)}, u32[]{:S(2)}) copy-start(f32[1,256]{1,0:T(1,128)} %get-tuple-element.5) | copy-start | bytes 3076

commit v5 on v4

--- a/solution.py
+++ b/solution.py
@@ -302,6 +302,16 @@
                 start_down(origin)
 
             rank_copy_in(origin).wait_recv()
+
+        return carry
+
+    def pack_event(e, carry):
+        distance = (e + 1) // 2
+        up = lax.rem(e, 2)
+        origin = z + jnp.where(up == 1, -distance, distance)
+
+        @pl.when(jnp.logical_and(origin >= 0, origin < N_Z))
+        def _():
             pack(origin, ranks[origin, 1])
             send_packed(origin)
 
@@ -318,6 +328,7 @@
         )
 
     lax.fori_loop(1, 3, event, 0)
+    lax.fori_loop(1, 3, pack_event, 0)
     pair_copy.wait_recv()
 
     def send_first(i, carry):
@@ -326,7 +337,10 @@
         return carry
 
     lax.fori_loop(0, N_Y - 1, send_first, 0)
-    lax.fori_loop(3, 2 * N_Z - 1, event, 0)
+    lax.fori_loop(3, 5, event, 0)
+    lax.fori_loop(3, 5, pack_event, 0)
+    lax.fori_loop(5, 7, event, 0)
+    lax.fori_loop(5, 7, pack_event, 0)
     pl.semaphore_wait(vouched, 1)
 
     left_four = lax.broadcasted_iota(jnp.int32, (N_Z, 128), 1) < CAP
@@ -409,6 +423,27 @@
         mean = jnp.sum(squares, axis=1, keepdims=True) / D
         scale = jnp.where(sweep == 0, 1.0, lax.rsqrt(mean + EPSILON))
         return scale * lax.rsqrt(mean * scale * scale + EPSILON)
+
+    def leave_origin(origin, carry):
+        def step(i, inner):
+            row_copy(origin, i).wait_send()
+            return inner
+
+        lax.fori_loop(0, LAYER - 1, step, 0)
+
+        @pl.when(jnp.logical_and(origin <= z, z < N_Z - 1))
+        def _():
+            unit_copy(origin, 1).wait_send()
+
+        @pl.when(jnp.logical_and(origin >= z, z > 0))
+        def _():
+            unit_copy(origin, 0).wait_send()
+
+        @pl.when(origin != z)
+        def _():
+            rank_copy(origin).wait_send()
+
+        return carry
 
     def sweep_step(sweep, carry):
         def unit_half(h):
@@ -562,6 +597,18 @@
 
         lax.fori_loop(0, N_DP - 1, send_second, 0)
 
+        for ref, sem, count in (
+            (part_in, part_send, LAYER - 1),
+            (line_in, line_send, N_Z - 1),
+            (total_in, total_send, LAYER - 1),
+        ):
+            sent = ref.at[sweep, pl.ds(0, count)]
+            pltpu.make_async_copy(sent, sent, sem.at[sweep]).wait()
+
+        @pl.when(sweep == 0)
+        def _():
+            lax.fori_loop(0, N_Z, leave_origin, 0)
+
         for h in range(2):
             panel_in[sweep, h, dp] = panel_out[sweep, h, dp]
             seen = panel_in.at[sweep, h, pl.ds(0, N_DP - 1)]
@@ -608,20 +655,10 @@
         out_ref[:, half * h : half * (h + 1)] = last_sums[h] * scales
         mass_ref[:, half * h : half * (h + 1)] = edges[1:2]
 
-    def leave(sweep, carry):
-        for ref, sem, count in (
-            (part_in, part_send, LAYER - 1),
-            (line_in, line_send, N_Z - 1),
-            (total_in, total_send, LAYER - 1),
-        ):
-            sent = ref.at[sweep, pl.ds(0, count)]
-            pltpu.make_async_copy(sent, sent, sem.at[sweep]).wait()
+    for sweep in range(ITERS):
         for h in range(2):
             sent = panel_in.at[sweep, h, pl.ds(0, N_DP - 1)]
             pltpu.make_async_copy(sent, sent, panel_send.at[sweep, h]).wait()
-        return carry
-
-    lax.fori_loop(0, ITERS, leave, 0)
     for h in range(2):
         sent = fresh.at[1, h, pl.ds(0, N_DP - 1)]
         pltpu.make_async_copy(sent, sent, fresh_send.at[h]).wait()
@@ -630,29 +667,6 @@
     pair_copy.wait_send()
     sent = fresh.at[0, :, pl.ds(0, 2 * (N_Y - 1))]
     pltpu.make_async_copy(sent, sent, first_sems.at[0]).wait()
-
-    def leave_origin(origin, carry):
-        def step(i, inner):
-            row_copy(origin, i).wait_send()
-            return inner
-
-        lax.fori_loop(0, LAYER - 1, step, 0)
-
-        @pl.when(jnp.logical_and(origin <= z, z < N_Z - 1))
-        def _():
-            unit_copy(origin, 1).wait_send()
-
-        @pl.when(jnp.logical_and(origin >= z, z > 0))
-        def _():
-            unit_copy(origin, 0).wait_send()
-
-        @pl.when(origin != z)
-        def _():
-            rank_copy(origin).wait_send()
-
-        return carry
-
-    lax.fori_loop(0, N_Z, leave_origin, 0)
 
 
 def body(vectors, candidates, centroids):

time: 148 us -> 147 us (level)
  no operation moved by 1% of the time
where the time goes in v5:
time: 147 us; the launch traced here: 146 us
  Pallas kernels  144 us (98%)
  local copies, waits for them, and re-layouts  2.04 us (1%)
    pallas_call x1, Pallas kernels, body(): pl.pallas_call(kernel, out_shape=(jax.ShapeDtypeStruct((PANEL, BLOCK), F3...  144 us

profile of v5, /device:TPU:8, one launch (start us, length us, event | category | flops | bytes accessed | tf_op | source)
XLA Modules:
  0.0 146.5 jit_solution(12507219210160824291)
XLA Ops:
  0.6 143.8 %soft_kmeans.1 = (f32[64,256]{1,0:T(8,128)}, f32[1,256]{1,0:T(1,128)}) custom-call(bf16[256,1024]{1,0:T(8,128)(2,1)} %vec_hbm.1, s32[4,256]{1,0:T(4,128)} %bitcast.7, bf16[64,256]{1,0:T(8,128)(2,1)} %bitcast.6), custom_call_target="tpu_custom_call" | custom-call | flops 4831838208 | bytes 4194304 | tf_op jit(solution)/shard_map/soft_kmeans/pallas_call | solution.py:675
  144.4 0.0 copy-start
  144.5 1.5 %copy.7 = f32[256,64]{0,1:T(8,128)} copy(f32[256,64]{0,1:T(8,128)} %bitcast.4) | data formatting | bytes 131072
  145.9 0.0 copy-done
  145.9 0.6 copy.8
Async XLA Ops:
  144.4 1.5 %copy-start = (f32[1,256]{1,0:T(1,128)S(1)}, f32[1,256]{1,0:T(1,128)}, u32[]{:S(2)}) copy-start(f32[1,256]{1,0:T(1,128)} %get-tuple-element.5) | copy-start | bytes 3076

commit v6 on v5

--- a/solution.py
+++ b/solution.py
@@ -145,12 +145,39 @@
     ]
     for fetch in fetches:
         fetch.start()
-    for fetch in fetches:
-        fetch.wait()
-
+
+    fetches[0].wait()
     vec = vec_ref[...].astype(F32)
     vec_scale = lax.rsqrt(jnp.mean(vec * vec, axis=1, keepdims=True) + EPSILON)
     units[z] = (vec * vec_scale).astype(BF16)
+
+    pl.semaphore_wait(barrier, LAYER - 1 + N_Z - 1 + N_Y)
+    pl.semaphore_signal(vouched, inc=1, device_id=(other_dp, cent), device_id_type=MESH)
+
+    def unit_copy(origin, side):
+        return pltpu.make_async_remote_copy(
+            src_ref=units.at[origin],
+            dst_ref=units.at[origin],
+            send_sem=z_send.at[origin, side],
+            recv_sem=z_recv.at[origin],
+            device_id=at_layer(z + 2 * side - 1),
+            device_id_type=MESH,
+        )
+
+    def start_up(origin):
+        @pl.when(z < N_Z - 1)
+        def _():
+            unit_copy(origin, 1).start()
+
+    def start_down(origin):
+        @pl.when(z > 0)
+        def _():
+            unit_copy(origin, 0).start()
+
+    start_up(z)
+    start_down(z)
+
+    fetches[1].wait()
     cand = cand_ref[...]
     place = lax.broadcasted_iota(jnp.int32, (N_CENT, ROWS), 0)
     block = ((place >> 1) & (N_X - 1)) * LAYER + (place >> 3) * 2 + (place & 1)
@@ -181,6 +208,65 @@
         packed[origin] = chosen.astype(BF16).reshape(LAYER, CAP, D)
         rows[origin * LAYER + seat] = packed[origin, seat]
 
+    pack(z, ranks[z, 0])
+
+    def rank_copy(layer):
+        return pltpu.make_async_remote_copy(
+            src_ref=ranks.at[layer, 0],
+            dst_ref=ranks.at[z, 1],
+            send_sem=rank_send.at[layer],
+            recv_sem=rank_recv.at[z],
+            device_id=at_layer(layer),
+            device_id_type=MESH,
+        )
+
+    def send_rank(i, carry):
+        rank_copy(z_peer(i)).start()
+        return carry
+
+    lax.fori_loop(1, N_Z, send_rank, 0)
+
+    def first_copy(which, i):
+        return pltpu.make_async_remote_copy(
+            src_ref=fresh.at[0, :, which],
+            dst_ref=fresh.at[0, :, which],
+            send_sem=first_sems.at[0],
+            recv_sem=first_sems.at[1],
+            device_id=(y_peer(i), cent),
+            device_id_type=MESH,
+        )
+
+    def fresh_copy(sweep, h, i):
+        return pltpu.make_async_remote_copy(
+            src_ref=fresh.at[sweep, h, dp],
+            dst_ref=fresh.at[sweep, h, dp],
+            send_sem=fresh_send.at[h],
+            recv_sem=fresh_recv.at[h],
+            device_id=(dp_peer(i), cent),
+            device_id_type=MESH,
+        )
+
+    def row_copy(origin, i):
+        target = seat_peer(i)
+        return pltpu.make_async_remote_copy(
+            src_ref=packed.at[origin, target],
+            dst_ref=rows.at[origin * LAYER + seat],
+            send_sem=x_send.at[origin, target],
+            recv_sem=x_recv.at[origin * LAYER + seat],
+            device_id=at_seat(target),
+            device_id_type=MESH,
+        )
+
+    def send_packed(origin):
+        def step(i, carry):
+            row_copy(origin, i).start()
+            return carry
+
+        lax.fori_loop(0, LAYER - 1, step, 0)
+
+    send_packed(z)
+
+    fetches[2].wait()
     half = BLOCK // 2
     quarter = half // 2
     left = lax.broadcasted_iota(jnp.int32, (quarter, 128), 1) < PANEL
@@ -188,11 +274,6 @@
         across = cent_ref[:, half * h : half * (h + 1)].astype(F32)
         along = jnp.transpose(jnp.concatenate([across, across], axis=0))
         fresh[0, h, dp] = jnp.where(left, along[:quarter], along[quarter:]).astype(BF16)
-
-    pack(z, ranks[z, 0])
-
-    pl.semaphore_wait(barrier, LAYER - 1 + N_Z - 1 + N_Y)
-    pl.semaphore_signal(vouched, inc=1, device_id=(other_dp, cent), device_id_type=MESH)
 
     pair_copy = pltpu.make_async_remote_copy(
         src_ref=fresh.at[0, :, dp],
@@ -203,86 +284,6 @@
         device_id_type=MESH,
     )
     pair_copy.start()
-
-    def rank_copy(layer):
-        return pltpu.make_async_remote_copy(
-            src_ref=ranks.at[layer, 0],
-            dst_ref=ranks.at[z, 1],
-            send_sem=rank_send.at[layer],
-            recv_sem=rank_recv.at[z],
-            device_id=at_layer(layer),
-            device_id_type=MESH,
-        )
-
-    def unit_copy(origin, side):
-        return pltpu.make_async_remote_copy(
-            src_ref=units.at[origin],
-            dst_ref=units.at[origin],
-            send_sem=z_send.at[origin, side],
-            recv_sem=z_recv.at[origin],
-            device_id=at_layer(z + 2 * side - 1),
-            device_id_type=MESH,
-        )
-
-    def start_up(origin):
-        @pl.when(z < N_Z - 1)
-        def _():
-            unit_copy(origin, 1).start()
-
-    def start_down(origin):
-        @pl.when(z > 0)
-        def _():
-            unit_copy(origin, 0).start()
-
-    start_up(z)
-    start_down(z)
-
-    def send_rank(i, carry):
-        rank_copy(z_peer(i)).start()
-        return carry
-
-    lax.fori_loop(1, N_Z, send_rank, 0)
-
-
-    def first_copy(which, i):
-        return pltpu.make_async_remote_copy(
-            src_ref=fresh.at[0, :, which],
-            dst_ref=fresh.at[0, :, which],
-            send_sem=first_sems.at[0],
-            recv_sem=first_sems.at[1],
-            device_id=(y_peer(i), cent),
-            device_id_type=MESH,
-        )
-
-    def fresh_copy(sweep, h, i):
-        return pltpu.make_async_remote_copy(
-            src_ref=fresh.at[sweep, h, dp],
-            dst_ref=fresh.at[sweep, h, dp],
-            send_sem=fresh_send.at[h],
-            recv_sem=fresh_recv.at[h],
-            device_id=(dp_peer(i), cent),
-            device_id_type=MESH,
-        )
-
-    def row_copy(origin, i):
-        target = seat_peer(i)
-        return pltpu.make_async_remote_copy(
-            src_ref=packed.at[origin, target],
-            dst_ref=rows.at[origin * LAYER + seat],
-            send_sem=x_send.at[origin, target],
-            recv_sem=x_recv.at[origin * LAYER + seat],
-            device_id=at_seat(target),
-            device_id_type=MESH,
-        )
-
-    def send_packed(origin):
-        def step(i, carry):
-            row_copy(origin, i).start()
-            return carry
-
-        lax.fori_loop(0, LAYER - 1, step, 0)
-
-    send_packed(z)
 
     def event(e, carry):
         distance = (e + 1) // 2

time: 147 us -> 146 us (level)
  no operation moved by 1% of the time
where the time goes in v6:
time: 146 us
  Pallas kernels  143 us (98%)
  local copies, waits for them, and re-layouts  2.04 us (1%)
    pallas_call x1, Pallas kernels, body(): pl.pallas_call(kernel, out_shape=(jax.ShapeDtypeStruct((PANEL, BLOCK), F3...  143 us

profile of v6, /device:TPU:8, one launch (start us, length us, event | category | flops | bytes accessed | tf_op | source)
XLA Modules:
  0.0 145.9 jit_solution(17257476858894286790)
XLA Ops:
  0.6 143.2 %soft_kmeans.1 = (f32[64,256]{1,0:T(8,128)}, f32[1,256]{1,0:T(1,128)}) custom-call(bf16[256,1024]{1,0:T(8,128)(2,1)} %vec_hbm.1, s32[4,256]{1,0:T(4,128)} %bitcast.7, bf16[64,256]{1,0:T(8,128)(2,1)} %bitcast.6), custom_call_target="tpu_custom_call" | custom-call | flops 4831838208 | bytes 4194304 | tf_op jit(solution)/shard_map/soft_kmeans/pallas_call | solution.py:676
  143.9 0.0 copy-start
  143.9 1.5 %copy.7 = f32[256,64]{0,1:T(8,128)} copy(f32[256,64]{0,1:T(8,128)} %bitcast.4) | data formatting | bytes 131072
  145.4 0.0 copy-done
  145.4 0.6 copy.8
Async XLA Ops:
  143.9 1.5 %copy-start = (f32[1,256]{1,0:T(1,128)S(1)}, f32[1,256]{1,0:T(1,128)}, u32[]{:S(2)}) copy-start(f32[1,256]{1,0:T(1,128)} %get-tuple-element.5) | copy-start | bytes 3076

commit v7 on v6

--- a/solution.py
+++ b/solution.py
@@ -17,6 +17,7 @@
 CAP = 64
 N_DP = 16
 N_CENT = 32
+EARLY = 4
 N_X = 4
 N_Y = 8
 N_Z = 4
@@ -174,8 +175,10 @@
         def _():
             unit_copy(origin, 0).start()
 
-    start_up(z)
-    start_down(z)
+    @pl.when(core == 0)
+    def _():
+        start_up(z)
+        start_down(z)
 
     fetches[1].wait()
     cand = cand_ref[...]
@@ -266,6 +269,13 @@
 
     send_packed(z)
 
+    @pl.when(core == 1)
+    def _():
+        for i in range(EARLY):
+            row_copy(z, i).wait_send()
+        start_up(z)
+        start_down(z)
+
     fetches[2].wait()
     half = BLOCK // 2
     quarter = half // 2
@@ -427,7 +437,10 @@
 
     def leave_origin(origin, carry):
         def step(i, inner):
-            row_copy(origin, i).wait_send()
+            @pl.when(jnp.logical_or(i >= EARLY, jnp.logical_or(origin != z, core == 0)))
+            def _():
+                row_copy(origin, i).wait_send()
+
             return inner
 
         lax.fori_loop(0, LAYER - 1, step, 0)

time: 146 us -> 150 us (1.027)
  Pallas kernels: 143 us -> 147 us
    pallas_call x1, Pallas kernels: 143 us -> 147 us  [body(): pl.pallas_call(kernel, out_shape=(jax.ShapeDtypeStruct((PANEL, BLOCK), F3...]
where the time goes in v7:
time: 150 us
  Pallas kernels  147 us (98%)
  local copies, waits for them, and re-layouts  2.04 us (1%)
    pallas_call x1, Pallas kernels, body(): pl.pallas_call(kernel, out_shape=(jax.ShapeDtypeStruct((PANEL, BLOCK), F3...  147 us

profile of v7, /device:TPU:8, one launch (start us, length us, event | category | flops | bytes accessed | tf_op | source)
XLA Modules:
  0.0 149.8 jit_solution(15057262414535998282)
XLA Ops:
  0.6 147.1 %soft_kmeans.1 = (f32[64,256]{1,0:T(8,128)}, f32[1,256]{1,0:T(1,128)}) custom-call(bf16[256,1024]{1,0:T(8,128)(2,1)} %vec_hbm.1, s32[4,256]{1,0:T(4,128)} %bitcast.7, bf16[64,256]{1,0:T(8,128)(2,1)} %bitcast.6), custom_call_target="tpu_custom_call" | custom-call | flops 4831838208 | bytes 4194304 | tf_op jit(solution)/shard_map/soft_kmeans/pallas_call | solution.py:689
  147.8 0.0 copy-start
  147.8 1.5 copy.7
  149.2 0.0 copy-done
  149.3 0.6 copy.8
Async XLA Ops:
  147.8 1.5 copy-start
